TPU v7x, 512 devices: a whole 4x4x16 slice. The times are simulated.
512 devices in a mesh: dp: 64 (over x, z), proto: 8 (over y, core).
Axes of the slice: x: 4, y: 4, z: 16, core: 2. Of those that a mesh axis runs over, the one named last changes fastest.
Arguments:
- student_hidden: bfloat16 [16384, 2048], P('dp', 'proto'), may hold values from -1 to 2.5
- teacher_hidden: bfloat16 [16384, 2048], P('dp', 'proto'), may hold values from -1 to 2.5
- mask_index: int32 [64, 128], P('dp'), may hold values from 0 to 255, as said below
- mask_count: int32 [64], P('dp'), may hold values from 26 to 128, as said below
- student_bottle: bfloat16 [2048, 256], P('proto'), may hold values from -1.5 to 1.5
- teacher_bottle: bfloat16 [2048, 256], P('proto'), may hold values from -1.5 to 1.5
- student_protos: bfloat16 [65536, 256], P(('dp', 'proto')), may hold values from -2 to 2
- teacher_protos: bfloat16 [65536, 256], P(('dp', 'proto')), may hold values from -2 to 2
Outputs:
- token_loss: float32 [8192], P('dp')
- proto_grad: float32 [65536, 256], P(('dp', 'proto'))
- hidden_grad: bfloat16 [8192, 2048], P('dp', 'proto')
Inputs may be any that keep to these rules, and one draw needn't show every extreme that they name: `mask_index`: the 128 entries of an image are distinct patch numbers below 256. Image g's masked patches are its first mask_count[g] slots.
All inputs are finite; a program needn't handle non-finite values.
Results may differ from a plain program's by a relative error of at most 0.02.
Values may be sent and summed in bfloat16 or wider, within the bound.
A program may use at most 64 MiB of HBM per device.

v0:
```python
import jax
import jax.numpy as jnp
from jax import lax
from jax.sharding import PartitionSpec as P

ITERS = 3


TEACHER_TEMP = 0.07
STUDENT_TEMP = 0.1
GRAD_SCALE = 16777216.0
EPSILON = 1e-06


def unit_rows(vectors):
    length = jnp.sqrt(jnp.sum(vectors * vectors, axis=1, keepdims=True) + EPSILON)
    return (vectors / length, length)


def contract_last(left, right):
    return lax.dot_general(
        left, right, (((1,), (1,)), ((), ())), preferred_element_type=jnp.float32
    )


def body(
    student_hidden,
    teacher_hidden,
    mask_index,
    mask_count,
    student_bottle,
    teacher_bottle,
    student_protos,
    teacher_protos,
):
    img_dev, mask_max = mask_index.shape
    patches = student_hidden.shape[0] // img_dev
    images = img_dev * lax.axis_size("dp")
    own_rows = student_protos.shape[0]
    image_base = jnp.arange(img_dev, dtype=jnp.int32)[:, None] * patches
    slot_rows = (image_base + mask_index).reshape(-1)
    slot_index = jnp.arange(mask_max, dtype=jnp.int32)[None, :]
    live_slots = (slot_index < mask_count[:, None]).astype(jnp.float32).reshape(-1)
    token_weight = (
        live_slots.reshape(img_dev, mask_max) / (mask_count[:, None].astype(jnp.float32) * images)
    ).reshape(-1)
    student_slots = jnp.take(student_hidden, slot_rows, axis=0)
    teacher_slots = jnp.take(teacher_hidden, slot_rows, axis=0)
    student_part = jnp.dot(student_slots, student_bottle, preferred_element_type=jnp.float32)
    teacher_part = jnp.dot(teacher_slots, teacher_bottle, preferred_element_type=jnp.float32)
    student_z, teacher_z = lax.psum((student_part, teacher_part), "proto")
    student_unit, student_len = unit_rows(student_z)
    student_unit = student_unit.astype(jnp.bfloat16)
    teacher_unit = unit_rows(teacher_z)[0].astype(jnp.bfloat16)
    student_rows, teacher_rows = (
        lax.all_gather(student_protos, "dp", axis=0, tiled=True),
        lax.all_gather(teacher_protos, "dp", axis=0, tiled=True),
    )
    student_dir, student_norm = unit_rows(student_rows.astype(jnp.float32))
    student_dir = student_dir.astype(jnp.bfloat16)
    teacher_dir = unit_rows(teacher_rows.astype(jnp.float32))[0].astype(jnp.bfloat16)
    own_norm = lax.dynamic_slice_in_dim(student_norm, lax.axis_index("dp") * own_rows, own_rows, 0)
    own_raw = student_protos.astype(jnp.float32)
    student_logits = contract_last(student_unit, student_dir)
    plan = live_slots[:, None] * jnp.exp(contract_last(teacher_unit, teacher_dir) / TEACHER_TEMP)
    student_exp = jnp.exp(student_logits / STUDENT_TEMP)
    for sweep_index in range(ITERS):
        proto_total = lax.psum(jnp.sum(plan, axis=0), "dp")
        plan = plan * (1.0 / proto_total)[None, :]
        if sweep_index + 1 < ITERS:
            token_total = lax.psum(jnp.sum(plan, axis=1), "proto")
            plan = plan * (1.0 / jnp.where(live_slots > 0, token_total, 1.0))[:, None]
    part_z = jnp.sum(student_exp, axis=1)
    token_total = lax.psum(jnp.sum(plan, axis=1), "proto")
    plan = plan * (1.0 / jnp.where(live_slots > 0, token_total, 1.0))[:, None]
    total_z, total_ts = lax.psum((part_z, jnp.sum(plan * student_logits, axis=1)), "proto")
    token_loss = live_slots * (jnp.log(total_z) - total_ts / STUDENT_TEMP)
    d_logits = (
        GRAD_SCALE * token_weight[:, None] * (student_exp / total_z[:, None] - plan) / STUDENT_TEMP
    ).astype(jnp.bfloat16)
    unit_grad = lax.psum(
        jnp.dot(d_logits, student_dir, preferred_element_type=jnp.float32).astype(jnp.bfloat16),
        "proto",
    ).astype(jnp.float32)
    bottle_grad = (
        unit_grad / student_len
        - student_z * jnp.sum(student_z * unit_grad, axis=1, keepdims=True) / student_len**3
    ).astype(jnp.bfloat16)
    hidden_grad = contract_last(bottle_grad, student_bottle).astype(jnp.bfloat16)
    received = lax.all_to_all(d_logits, "dp", split_axis=1, concat_axis=0, tiled=True)
    raw_grad = lax.dot_general(
        received,
        lax.all_gather(student_unit, "dp", axis=0, tiled=True),
        (((0,), (0,)), ((), ())),
        preferred_element_type=jnp.float32,
    )
    proto_grad = (
        raw_grad / own_norm
        - own_raw * jnp.sum(own_raw * raw_grad, axis=1, keepdims=True) / own_norm**3
    )
    return (token_loss, proto_grad, hidden_grad)


def solution(mesh):
    placed = (
        P("dp", "proto"),
        P("dp", "proto"),
        P("dp", None),
        P("dp"),
        P("proto", None),
        P("proto", None),
        P(("dp", "proto"), None),
        P(("dp", "proto"), None),
    )
    return jax.shard_map(
        body,
        mesh=mesh,
        in_specs=placed,
        out_specs=(P("dp"), P(("dp", "proto"), None), P("dp", "proto")),
        check_vma=False,
    )
```

profile of v0, /device:TPU:1, one launch (start us, length us, event | category | flops | bytes accessed | tf_op | source)
XLA Modules:
  0.0 1248.9 jit_solution(7996136784671859071)
XLA Ops:
  8.0 0.0 all-reduce.7.cloned.1.call-start
  8.1 0.7 compare_select_fusion
  8.7 0.7 compare_and_fusion
  9.4 1.7 gather_fusion
  11.1 1.7 gather_fusion.1
  12.8 0.9 fusion.19
  13.7 1.8 fusion.17
  15.4 0.0 all-gather.6.cloned.1.call-start
  15.5 0.5 all-gather.6.cloned.1.call-update
  16.0 0.0 all-gather.4.cloned.1.call-start
  16.1 0.5 all-gather.4.cloned.1.call-update
  16.6 0.0 all-reduce.5.cloned.1.call-start
  17.4 78.2 %all-reduce.7.cloned.1.call-done = (f32[128,256]{1,0:T(8,128)}, f32[128,256]{1,0:T(8,128)}) async-done(((f32[128,256]{1,0:T(8,128)}, f32[128,256]{1,0:T(8,128)}), (f32[128,256]{1,0:T(8,128)}, f32[128,256]{1,0:T(8,128)})) %all-reduce.7.cloned.1.call-update) | async-done | bytes 262160 | tf_op jit(solution)/shard_map/psum | solution.py:51
  95.6 1.1 multiply_reduce_fusion.4
  96.7 1.0 multiply_reduce_fusion.5
  97.7 1.0 divide_convert_fusion.1
  98.7 63.2 %all-gather.6.cloned.1.call-done = bf16[8192,256]{1,0:T(8,128)(2,1)} async-done(((bf16[128,256]{1,0:T(8,128)(2,1)}), bf16[8192,256]{1,0:T(8,128)(2,1)}) %all-gather.6.cloned.1.call-update) | async-done | bytes 4194320 | tf_op jit(solution)/shard_map/all_gather | solution.py:57
  161.9 3.5 fusion.4
  165.5 3.5 fusion.34
  169.0 222.4 %psum.80 = f32[8192]{0:T(1024)S(1)} all-reduce(f32[8192]{0:T(1024)S(1)} %get-tuple-element.14), channel_id=1, replica_groups=mesh['dp'=64,'proto'=8] {'dp'}, use_global_device_ids=true, to_apply=%region_9.11 | all-reduce | flops 8192 | bytes 65536 | tf_op jit(solution)/shard_map/psum | solution.py:68
  391.4 2.5 multiply_reduce_fusion.3
  394.0 76.1 %psum.81 = f32[128]{0:T(128)S(1)} all-reduce(f32[128]{0:T(128)S(1)} %multiply_reduce_fusion.3), channel_id=1, replica_groups=mesh['dp'=64,'proto'=8] {'proto'}, use_global_device_ids=true, to_apply=%region_11.13 | all-reduce | flops 128 | bytes 1024 | tf_op jit(solution)/shard_map/psum | solution.py:71
  470.1 2.7 multiply_reduce_fusion.2
  472.8 218.9 %psum.82 = f32[8192]{0:T(1024)S(1)} all-reduce(f32[8192]{0:T(1024)S(1)} %multiply_reduce_fusion.2), channel_id=1, replica_groups=mesh['dp'=64,'proto'=8] {'dp'}, use_global_device_ids=true, to_apply=%region_13.15 | all-reduce | flops 8192 | bytes 65536 | tf_op jit(solution)/shard_map/psum | solution.py:68
  691.7 2.9 fusion.33
  694.7 67.4 %psum.83 = f32[128]{0:T(128)S(1)} all-reduce(f32[128]{0:T(128)S(1)} %fusion.33), channel_id=1, replica_groups=mesh['dp'=64,'proto'=8] {'proto'}, use_global_device_ids=true, to_apply=%region_15.17 | all-reduce | flops 128 | bytes 1024 | tf_op jit(solution)/shard_map/psum | solution.py:71
  762.1 3.0 multiply_reduce_fusion.1
  765.1 218.9 %psum.84 = f32[8192]{0:T(1024)S(1)} all-reduce(f32[8192]{0:T(1024)S(1)} %multiply_reduce_fusion.1), channel_id=1, replica_groups=mesh['dp'=64,'proto'=8] {'dp'}, use_global_device_ids=true, to_apply=%region_17.19 | all-reduce | flops 8192 | bytes 65536 | tf_op jit(solution)/shard_map/psum | solution.py:68
  984.0 3.2 fusion.9
  987.3 67.6 %psum.85 = f32[128]{0:T(128)S(1)} all-reduce(f32[128]{0:T(128)S(1)} %fusion.9), channel_id=1, replica_groups=mesh['dp'=64,'proto'=8] {'proto'}, use_global_device_ids=true, to_apply=%region_19.21 | all-reduce | flops 128 | bytes 1024 | tf_op jit(solution)/shard_map/psum | solution.py:74
  1054.9 3.5 fusion.2
  1058.5 3.5 fusion.3
  1062.0 4.2 fusion.8
  1066.2 12.4 all-reduce
  1078.6 4.6 multiply_convert_fusion
  1083.3 1.4 convolution_convert_fusion
  1084.7 0.0 all-gather.8.cloned.1.call-start
  1084.7 0.5 all-gather.8.cloned.1.call-update
  1085.3 1.9 copy_bitcast_fusion
  1087.2 4.7 all-to-all-start
  1091.9 0.1 fusion.29
  1092.0 0.5 subtract_select_fusion
  1092.5 52.5 %all-reduce.5.cloned.1.call-done = bf16[128,256]{1,0:T(8,128)(2,1)} async-done(((bf16[128,256]{1,0:T(8,128)(2,1)}), bf16[128,256]{1,0:T(8,128)(2,1)}) %all-reduce.5.cloned.1.call-update) | async-done | bytes 65552 | tf_op jit(solution)/shard_map/psum | solution.py:81
  1145.1 0.9 fusion.15
  1146.0 1.7 convolution_convert_fusion.1
  1147.7 89.7 %all-gather.8.cloned.1.call-done = bf16[8192,256]{1,0:T(8,128)(2,1)} async-done(((bf16[128,256]{1,0:T(8,128)(2,1)}), bf16[8192,256]{1,0:T(8,128)(2,1)}) %all-gather.8.cloned.1.call-update) | async-done | bytes 4194320 | tf_op jit(solution)/shard_map/all_gather | solution.py:93
  1237.4 3.1 fusion.10
  1240.5 0.8 fusion.12
  (37 shorter events, 0.2 us)
Async XLA Ops:
  8.0 4.8 copy-start
  8.0 87.6 %all-reduce.7.cloned.1.call-start = ((), (), s32[]{:S(2)}) async-start(), calls=%async_computation.5 | async-start | bytes 524288 | tf_op jit(solution)/shard_map/psum | solution.py:51
  15.4 146.5 %all-gather.6.cloned.1.call-start = ((), (), s32[]{:S(2)}) async-start(), calls=%async_computation.2 | async-start | bytes 4259840 | tf_op jit(solution)/shard_map/all_gather | solution.py:57
  16.0 1038.9 %all-gather.4.cloned.1.call-start = ((), (), s32[]{:S(2)}) async-start(), calls=%async_computation.1 | async-start | bytes 4259840 | tf_op jit(solution)/shard_map/all_gather | solution.py:56
  16.6 1128.4 %all-reduce.5.cloned.1.call-start = ((), (), s32[]{:S(2)}) async-start(), calls=%async_computation.4 | async-start | bytes 131072 | tf_op jit(solution)/shard_map/psum | solution.py:81
  95.6 69.9 %copy-start.9 = (f32[128,256]{1,0:T(8,128)S(1)}, f32[128,256]{1,0:T(8,128)}, u32[]{:S(2)}) copy-start(f32[128,256]{1,0:T(8,128)} %get-tuple-element.9) | copy-start | bytes 393220
  98.7 963.2 %copy-start.8 = (bf16[128,256]{1,0:T(8,128)(2,1)}, bf16[128,256]{1,0:T(8,128)(2,1)S(1)}, u32[]{:S(2)}) copy-start(bf16[128,256]{1,0:T(8,128)(2,1)S(1)} %divide_convert_fusion.1) | copy-start | bytes 196612
  161.9 3.5 copy-start.5
  1054.9 3.5 copy-start.2
  1058.4 3.5 copy-start.1
  1062.0 4.2 copy-start.3
  1078.6 4.7 copy-start.4
  1084.7 152.7 %all-gather.8.cloned.1.call-start = ((), (), s32[]{:S(2)}) async-start(), calls=%async_computation.3 | async-start | bytes 4259840 | tf_op jit(solution)/shard_map/all_gather | solution.py:93
  1085.2 59.8 %copy-start.6 = (f32[128,256]{1,0:T(8,128)S(1)}, f32[128,256]{1,0:T(8,128)}, u32[]{:S(2)}) copy-start(f32[128,256]{1,0:T(8,128)} %get-tuple-element.8) | copy-start | bytes 393220
  1085.3 152.1 %copy-start.7 = (bf16[128,256]{1,0:T(8,128)(2,1)S(1)}, bf16[128,256]{1,0:T(8,128)(2,1)}, u32[]{:S(2)}) copy-start(bf16[128,256]{1,0:T(8,128)(2,1)} %param.16) | copy-start | bytes 196612
  1087.2 150.2 %all-to-all-start = ((bf16[128,64,128]{2,0,1:T(8,128)(2,1)}), bf16[128,64,128]{2,0,1:T(8,128)(2,1)S(1)}, u32[]{:S(2)}, u32[]{:S(2)}) async-start(bf16[128,64,128]{2,0,1:T(8,128)(2,1)} %copy_bitcast_fusion), calls=%async_computation | async-start | bytes 4194304 | tf_op jit(solution)/shard_map/all_to_all | solution.py:90
Sparse Core Ops, SparseCore 0:
  15.6 79.9 all-reduce.6
  1084.8 60.2 all-reduce.4
Sparse Core Ops, SparseCore 1:
  18.9 143.0 all-gather.5
  165.2 141.9 all-gather.3
  1089.1 148.3 all-gather.7
where the time goes:
time: 1260 us; the launch traced here: 1250 us
  blocking collectives  884 us (70%)
  waiting for transfers between devices  285 us (23%)
  other arithmetic  36.4 us (3%)
  matrix products  16.6 us (1%)
  between operations  16.6 us (1%)
    psum x3, blocking collectives, body(): proto_total = lax.psum(jnp.sum(plan, axis=0), 'dp')  660 us
    psum x3, blocking collectives, body(): token_total = lax.psum(jnp.sum(plan, axis=1), 'proto')  211 us
    all_gather x1, waiting for transfers between devices, body(): lax.all_gather(student_unit, 'dp', axis=0, tiled=True)  89.7 us
    psum x1, waiting for transfers between devices, body(): student_z, teacher_z = lax.psum((student_part, teacher_part), 'proto')  78.2 us
    all_gather x1, waiting for transfers between devices, body(): lax.all_gather(teacher_protos, 'dp', axis=0, tiled=True)  63.2 us
    psum x1, waiting for transfers between devices, body(): lax.psum(jnp.dot(d_logits, student_dir, preferred_element_type=jnp.float3...  52.5 us
  transfers between devices with their start and end apart: 6, of which 4 were waited for; matrix products, arithmetic and copies ran while one was open for 2% of the time, Pallas kernels for 0%

commit v1 on v0

v1 whole, which is shorter than its diff:
```python
import functools
import math

import jax
import jax.numpy as jnp
from jax import lax
from jax.experimental import pallas as pl
from jax.experimental.pallas import tpu as pltpu
from jax.sharding import PartitionSpec as P

NZ = 16
NC = 2
ITERS = 3
TEACHER_TEMP = 0.07
STUDENT_TEMP = 0.1
GRAD_SCALE = 16777216.0
EPSILON = 1e-06
LOG2E = math.log2(math.e)
MESH = pl.DeviceIdType.MESH
F32 = jnp.float32
BF16 = jnp.bfloat16


def dot(a, b):
    return jnp.dot(a, b, preferred_element_type=F32)


def dot_last(a, b):
    return lax.dot_general(a, b, (((1,), (1,)), ((), ())), preferred_element_type=F32)


def unit_rows(v):
    length = jnp.sqrt(jnp.sum(v * v, axis=1, keepdims=True) + EPSILON)
    return v / length, length


def split_rows(row):
    wide = jnp.broadcast_to(row, (8, row.shape[1]))
    high = wide.astype(BF16).astype(F32)
    place = lax.broadcasted_iota(jnp.int32, wide.shape, 0)
    picked = jnp.where(place == 0, high, jnp.where(place == 1, wide - high, 0.0))
    return picked.astype(BF16)


def column(row):
    return jnp.broadcast_to(row, (128, row.shape[1])).T


def twice(col):
    return jnp.concatenate([col, col], axis=1)


def scratch_of(d):
    nx, ny, np_, nv, own, tok, half, nq = (
        d["nx"], d["ny"], d["np"], d["nv"], d["own"], d["tok"], d["half"], d["nq"],
    )
    bot, rows = d["bot"], d["rows"]
    vmem = {
        "zs_s": ((np_, own, bot), F32),
        "zs_t": ((np_, own, bot), F32),
        "zr_s": ((np_, own, bot), F32),
        "zr_t": ((np_, own, bot), F32),
        "zlen": ((own, 128), F32),
        "zown": ((own, bot), F32),
        "cnt": ((NZ, 1, 128), F32),
        "un_s": ((NC, NZ, own, bot), BF16),
        "un_t": ((NC, NZ, own, bot), BF16),
        "su_tr": ((bot, tok), BF16),
        "di_s": ((nv, rows, bot), BF16),
        "di_t": ((nv, rows, bot), BF16),
        "kf": ((nq, tok, 256), F32),
        "kb": ((nq, tok, 256), BF16),
        "ef": ((nq, tok, 256), F32),
        "kl": ((nq, tok, 256), BF16),
        "pb": ((ITERS, nv, nq, 256), F32),
        "pv": ((nq, 256), F32),
        "tz": ((ITERS - 1, NZ, 1, tok), F32),
        "tc": ((ITERS - 1, NC, 1, tok), F32),
        "ez": ((NZ, 1, tok), F32),
        "ec": ((NC, 1, tok), F32),
        "fz": ((NZ, 2, tok), F32),
        "fc": ((NC, 2, tok), F32),
        "loss": ((tok, 128), F32),
        "lb": ((np_, own, 128), F32),
        "ug": ((NC, half, bot), F32),
        "ur": ((half, bot), F32),
        "us": ((NZ, own, bot), BF16),
        "uz": ((NZ, own, bot), BF16),
        "rs": ((nv, bot, rows), BF16),
        "rr": ((nv, bot, rows), BF16),
        "bg": ((np_, own, bot), BF16),
    }
    sems = [
        "zr_s", "zr_t", "cnt", "un_s", "un_t", "uc_s", "uc_t", "di_s", "di_t", "pb0", "pb1", "pb2",
        "tz0", "tz1", "tc0", "tc1", "ez", "ec", "fz", "fc", "lb", "ur", "uz", "rr", "bg",
    ]
    return vmem, sems


def kernel(d, *refs):
    nx, ny, np_, nv, own, tok, half, nq = (
        d["nx"], d["ny"], d["np"], d["nv"], d["own"], d["tok"], d["half"], d["nq"],
    )
    bot, rows, slots, patches, images = d["bot"], d["rows"], d["slots"], d["patches"], d["images"]
    sh, th, idx, count, sb, tb, sp, tp, loss_out, proto_out, hidden_out = refs[:11]
    vmem, sems = scratch_of(d)
    m = dict(zip(vmem, refs[11 : 11 + len(vmem)]))
    send_sem, recv_sem = refs[11 + len(vmem) :]
    number = {name: i for i, name in enumerate(sems)}

    dp, pr = lax.axis_index("dp"), lax.axis_index("proto")
    x, z, y, c = dp // NZ, lax.rem(dp, NZ), pr // NC, lax.rem(pr, NC)
    v = x * ny + y
    sibling = (dp, y * NC + (1 - c))
    z_order = sorted(range(1, NZ), key=lambda k: -min(k, NZ - k))
    z_peers = [lax.rem(z + k, NZ) for k in z_order]
    pr_peers = [lax.rem(pr + k, np_) for k in range(1, np_)]
    v_peers = []
    for k in range(nx):
        for j in range(ny):
            if k or j:
                v_peers.append((lax.rem(x + k, nx), lax.rem(y + j, ny)))

    def at_z(other):
        return (x * NZ + other, pr)

    def at_pr(other):
        return (dp, other)

    def at_v(other):
        return (other[0] * NZ + z, other[1] * NC + c)

    def push(name, src, dst, device):
        pltpu.make_async_remote_copy(
            src_ref=src,
            dst_ref=dst,
            send_sem=send_sem.at[number[name]],
            recv_sem=recv_sem.at[number[name]],
            device_id=device,
            device_id_type=MESH,
        ).start()

    sent = []

    def arrived(name, like):
        pltpu.make_async_copy(like, like, recv_sem.at[number[name]]).wait()
        sent.append((name, like))

    def to_z(name, src, dst):
        for other in z_peers:
            push(name, src, dst, at_z(other))

    def to_v(name, src, dst):
        for other in v_peers:
            push(name, src, dst, at_v(other))

    barrier = pltpu.get_barrier_semaphore()
    peers = [at_pr(o) for o in pr_peers] + [at_z(o) for o in z_peers]
    for k in range(nx):
        for j in range(ny):
            if k:
                peers.append(at_v((lax.rem(x + k, nx), lax.rem(y + j, ny))))
    for device in peers:
        pl.semaphore_signal(barrier, inc=1, device_id=device, device_id_type=MESH)

    picked = twice(jnp.broadcast_to(idx[...].astype(F32), (128, slots)).T)
    patch = lax.broadcasted_iota(jnp.int32, (slots, patches), 1).astype(F32)
    one_hot = jnp.where(picked == patch, 1.0, 0.0).astype(BF16)
    m["zs_t"][...] = dot(dot(one_hot, th[...]).astype(BF16), tb[...]).reshape(np_, own, bot)
    m["zs_s"][...] = dot(dot(one_hot, sh[...]).astype(BF16), sb[...]).reshape(np_, own, bot)
    m["di_t"][v] = unit_rows(tp[...].astype(F32))[0].astype(BF16)
    m["di_s"][v] = unit_rows(sp[...].astype(F32))[0].astype(BF16)
    m["cnt"][z] = jnp.full((1, 128), count[0].astype(F32), F32)

    pl.semaphore_wait(barrier, len(peers))
    for name in ("t", "s"):
        for other in pr_peers:
            push("zr_" + name, m["zs_" + name].at[other], m["zr_" + name].at[pr], at_pr(other))
        m["zr_" + name][pr] = m["zs_" + name][pr]
    to_z("cnt", m["cnt"].at[z], m["cnt"].at[z])
    to_v("di_t", m["di_t"].at[v], m["di_t"].at[v])
    to_v("di_s", m["di_s"].at[v], m["di_s"].at[v])

    for name in ("t", "s"):
        arrived("zr_" + name, m["zr_" + name].at[pl.ds(0, np_ - 1)])
        own_z = jnp.sum(m["zr_" + name][...], axis=0)
        unit, length = unit_rows(own_z)
        m["un_" + name][c, z] = unit.astype(BF16)
        mine = m["un_" + name].at[c, z]
        to_z("un_" + name, mine, mine)
        if name == "s":
            m["zown"][...] = own_z
            m["zlen"][...] = jnp.broadcast_to(length, (own, 128))

    arrived("cnt", m["cnt"].at[pl.ds(0, NZ - 1)])
    lane = lax.broadcasted_iota(jnp.int32, (1, tok), 1)
    lane_c, lane_z, lane_i = lane // half, lax.rem(lane, half) // own, lax.rem(lane, own)
    counts = jnp.zeros((1, tok), F32)
    for k in range(NZ):
        value = jnp.concatenate([m["cnt"][k]] * (tok // 128), axis=1)
        counts = jnp.where(lane_z == k, value, counts)
    slot = ((y * NC + lane_c) * own + lane_i).astype(F32)
    live = jnp.where(slot < counts, 1.0, 0.0)

    def whole_units(name):
        arrived("un_" + name, m["un_" + name].at[0, pl.ds(0, NZ - 1)])
        mine = m["un_" + name].at[c]
        push("uc_" + name, mine, mine, sibling)
        arrived("uc_" + name, m["un_" + name].at[0])

    def units(name):
        return m["un_" + name][...].reshape(tok, bot)

    def dirs(name, q):
        return m["di_" + name][pl.ds(2 * q, 2)].reshape(256, bot)

    whole_units("t")
    arrived("di_t", m["di_t"].at[pl.ds(0, nv - 1)])
    live_col = twice(column(live))

    def teacher(q, carry):
        logits = dot_last(units("t"), dirs("t", q))
        k_tile = live_col * jnp.exp2(logits * (LOG2E / TEACHER_TEMP))
        m["kf"][q] = k_tile
        m["kb"][q] = k_tile.astype(BF16)
        m["pb"][0, v, pl.ds(q, 1), :] = jnp.sum(k_tile, axis=0, keepdims=True)
        return carry

    lax.fori_loop(0, nq, teacher, 0)

    def send_p(k):
        mine = m["pb"].at[k, v]
        to_v("pb%d" % k, mine, mine)

    send_p(0)

    whole_units("s")
    arrived("di_s", m["di_s"].at[pl.ds(0, nv - 1)])
    m["su_tr"][...] = units("s").astype(F32).T.astype(BF16)
    ones = jnp.ones((8, 256), BF16)

    def student(q, total):
        logits = dot_last(units("s"), dirs("s", q))
        e_tile = jnp.exp2(logits * (LOG2E / STUDENT_TEMP))
        m["ef"][q] = e_tile
        m["kl"][q] = (m["kf"][q] * logits).astype(BF16)
        return total + dot_last(ones, e_tile.astype(BF16))

    e_sum = lax.fori_loop(0, nq, student, jnp.zeros((8, tok), F32))
    m["ez"][z] = e_sum[0:1]

    def over_p(which):
        def step(q, total):
            return total + dot_last(split_rows(m["pv"][pl.ds(q, 1), :]), m[which][q])

        total = lax.fori_loop(0, nq, step, jnp.zeros((8, tok), F32))
        return total[0:1] + total[1:2]

    def z_sum(name_z, name_c, z_buf, c_buf):
        arrived(name_z, z_buf.at[pl.ds(0, NZ - 1)])
        c_buf[c] = jnp.sum(z_buf[...], axis=0)
        push(name_c, c_buf.at[c], c_buf.at[c], sibling)

    def c_sum(name_c, c_buf):
        arrived(name_c, c_buf.at[0])
        return c_buf[0] + c_buf[1]

    for k in range(ITERS):
        arrived("pb%d" % k, m["pb"].at[k, pl.ds(0, nv - 1)])
        m["pv"][...] = 1.0 / jnp.sum(m["pb"][k], axis=0)
        if k == ITERS - 1:
            break
        z_buf, c_buf = m["tz"].at[k], m["tc"].at[k]
        z_buf[z] = over_p("kb")
        to_z("tz%d" % k, z_buf.at[z], z_buf.at[z])
        if k == 0:
            to_z("ez", m["ez"].at[z], m["ez"].at[z])
        z_sum("tz%d" % k, "tc%d" % k, z_buf, c_buf)
        total = c_sum("tc%d" % k, c_buf)
        t_rows = split_rows(1.0 / jnp.where(live > 0, total, 1.0))

        def over_t(q, carry):
            part = dot(t_rows, m["kb"][q])
            m["pb"][k + 1, v, pl.ds(q, 1), :] = part[0:1] + part[1:2]
            return carry

        lax.fori_loop(0, nq, over_t, 0)
        send_p(k + 1)
        if k == 0:
            z_sum("ez", "ec", m["ez"], m["ec"])

    m["fz"][z] = jnp.concatenate([over_p("kb"), over_p("kl")], axis=0)
    to_z("fz", m["fz"].at[z], m["fz"].at[z])
    total_z = c_sum("ec", m["ec"])
    weight = live * (GRAD_SCALE / STUDENT_TEMP) / (counts * images)
    e_col = twice(column(weight / total_z))
    z_sum("fz", "fc", m["fz"], m["fc"])
    last = c_sum("fc", m["fc"])
    t_row = 1.0 / jnp.where(live > 0, last[0:1], 1.0)
    total_ts = last[1:2] * t_row
    m["loss"][...] = column(live * (jnp.log(total_z) - total_ts / STUDENT_TEMP))
    k_col = twice(column(weight * t_row))

    m["lb"][pr] = m["loss"][pl.ds(pl.multiple_of((c * NZ + z) * own, own), own), :]
    for other in pr_peers:
        push("lb", m["lb"].at[pr], m["lb"].at[pr], at_pr(other))

    m["ug"][...] = jnp.zeros((NC, half, bot), F32)

    def grads(q, carry):
        targets = k_col * (m["kf"][q] * m["pv"][pl.ds(q, 1), :])
        d_tile = (e_col * m["ef"][q] - targets).astype(BF16)
        m["ug"][...] += dot(d_tile, dirs("s", q)).reshape(NC, half, bot)
        raw = dot(m["su_tr"][...], d_tile).astype(BF16)
        m["rs"][2 * q] = raw[:, :rows]
        m["rs"][2 * q + 1] = raw[:, rows:]
        return carry

    lax.fori_loop(0, nq, grads, 0)
    push("ur", m["ug"].at[1 - c], m["ur"], sibling)
    for other in v_peers:
        push("rr", m["rs"].at[other[0] * ny + other[1]], m["rr"].at[v], at_v(other))
    m["rr"][v] = m["rs"][v]
    arrived("ur", m["ur"])
    m["us"][...] = (m["ug"][c] + m["ur"][...]).astype(BF16).reshape(NZ, own, bot)
    for other in z_peers:
        push("uz", m["us"].at[other], m["uz"].at[z], at_z(other))
    m["uz"][z] = m["us"][z]
    arrived("uz", m["uz"].at[pl.ds(0, NZ - 1)])
    unit_grad = jnp.sum(m["uz"][...].astype(F32), axis=0)
    own_z, length = m["zown"][...], m["zlen"][:, 0:1]
    along = jnp.sum(own_z * unit_grad, axis=1, keepdims=True)
    m["bg"][pr] = (unit_grad / length - own_z * along / length**3).astype(BF16)
    for other in pr_peers:
        push("bg", m["bg"].at[pr], m["bg"].at[pr], at_pr(other))

    arrived("rr", m["rr"].at[pl.ds(0, nv - 1)])
    raw_grad = jnp.sum(m["rr"][...].astype(F32), axis=0).T
    own_raw = sp[...].astype(F32)
    norm = unit_rows(own_raw)[1]
    proto_out[...] = raw_grad / norm - own_raw * jnp.sum(own_raw * raw_grad, axis=1, keepdims=True) / norm**3

    arrived("lb", m["lb"].at[pl.ds(0, np_ - 1)])
    loss_out[...] = m["lb"][...].reshape(slots, 128).T[0:1]
    arrived("bg", m["bg"].at[pl.ds(0, np_ - 1)])
    hidden_out[...] = dot_last(m["bg"][...].reshape(slots, bot), sb[...]).astype(BF16)

    for name, like in sent:
        pltpu.make_async_copy(like, like, send_sem.at[number[name]]).wait()


def body(sh, th, idx, count, sb, tb, sp, tp):
    n_dp, n_pr = lax.axis_size("dp"), lax.axis_size("proto")
    d = {"nx": n_dp // NZ, "ny": n_pr // NC, "np": n_pr, "slots": idx.shape[1], "images": n_dp}
    d["nv"] = d["nx"] * d["ny"]
    d["own"] = d["slots"] // n_pr
    d["half"] = NZ * d["own"]
    d["tok"] = NC * d["half"]
    d["rows"], d["bot"] = sp.shape
    d["nq"] = d["nv"] * d["rows"] // 256
    d["patches"] = sh.shape[0]
    vmem, sems = scratch_of(d)
    vm = pl.BlockSpec(memory_space=pltpu.VMEM)
    loss, proto_grad, hidden_grad = pl.pallas_call(
        functools.partial(kernel, d),
        out_shape=(
            jax.ShapeDtypeStruct((1, d["slots"]), F32),
            jax.ShapeDtypeStruct(sp.shape, F32),
            jax.ShapeDtypeStruct((d["slots"], sb.shape[0]), BF16),
        ),
        in_specs=[vm, vm, vm, pl.BlockSpec(memory_space=pltpu.SMEM), vm, vm, vm, vm],
        out_specs=(vm, vm, vm),
        scratch_shapes=[pltpu.VMEM(shape, dtype) for shape, dtype in vmem.values()]
        + [pltpu.SemaphoreType.DMA((len(sems),)), pltpu.SemaphoreType.DMA((len(sems),))],
        compiler_params=pltpu.CompilerParams(
            collective_id=0, has_side_effects=True, vmem_limit_bytes=48 * 2**20
        ),
    )(sh, th, idx, count, sb, tb, sp, tp)
    return loss.reshape(-1), proto_grad, hidden_grad


def solution(mesh):
    placed = (
        P("dp", "proto"),
        P("dp", "proto"),
        P("dp", None),
        P("dp"),
        P("proto", None),
        P("proto", None),
        P(("dp", "proto"), None),
        P(("dp", "proto"), None),
    )
    return jax.shard_map(
        body,
        mesh=mesh,
        in_specs=placed,
        out_specs=(P("dp"), P(("dp", "proto"), None), P("dp", "proto")),
        check_vma=False,
    )
```

time: 1260 us -> 122 us (0.10)
  blocking collectives: 884 us -> 0 us
  waiting for transfers between devices: 285 us -> 0 us
  Pallas kernels: 0 us -> 113 us
  other arithmetic: 36.4 us -> 0 us
  matrix products: 16.6 us -> 0 us
  between operations: 16.6 us -> 1.33 us
    psum x7 -> x0, blocking collectives: 884 us -> none  [the longest x3 660 us: body(): proto_total = lax.psum(jnp.sum(plan, axis=0), 'dp')]
    all_gather x3 -> x0, waiting for transfers between devices: 153 us -> none  [the longest x1 89.7 us: body(): lax.all_gather(student_unit, 'dp', axis=0, tiled=True)]
    psum x2 -> x0, waiting for transfers between devices: 131 us -> none  [the longest x1 78.2 us: body(): student_z, teacher_z = lax.psum((student_part, teacher_part), 'proto')]
    pallas_call x0 -> x1, Pallas kernels: none -> 113 us  [body(): pl.pallas_call(functools.partial(kernel, d), out_shape=(jax.ShapeDtypeStr...]
    reduce_sum x10 -> x0, other arithmetic: 24.4 us -> none  [the longest x4 9.08 us: unit_rows(): jnp.sum(vectors * vectors, axis=1, keepdims=True) + EPSILON]
    dot_general x7 -> x0, matrix products: 16.6 us -> none  [the longest x3 9.44 us: contract_last(): lax.dot_general(left, right, (((1,), (1,)), ((), ())), preferred_element_...]
  transfers between devices with their start and end apart: 6 -> 0, of which waited for: 4 -> 0; matrix products, arithmetic and copies ran while one was open for 2% -> 0% of each run, Pallas kernels for 0% -> 0%
where the time goes in v1:
time: 122 us; the launch traced here: 121 us
  Pallas kernels  113 us (93%)
  local copies, waits for them, and re-layouts  7.09 us (6%)
  between operations  1.33 us (1%)
    pallas_call x1, Pallas kernels, body(): pl.pallas_call(functools.partial(kernel, d), out_shape=(jax.ShapeDtypeStr...  113 us
    unnamed x17, local copies, waits for them, and re-layouts  7.09 us

profile of v1, /device:TPU:1, one launch (start us, length us, event | category | flops | bytes accessed | tf_op | source)
XLA Modules:
  0.0 121.3 jit_solution(5576831017743194625)
XLA Ops:
  0.6 0.0 copy-start.6
  1.3 0.0 copy-done.6
  1.3 0.0 copy-start
  1.3 0.9 copy-done
  2.2 0.0 copy-start.1
  2.2 0.9 copy-done.1
  3.1 0.0 copy-start.2
  3.1 0.9 copy-done.2
  4.0 0.0 copy-start.3
  4.0 0.9 copy-done.3
  4.9 0.0 copy-start.4
  4.9 0.8 copy-done.4
  5.8 0.0 copy-start.5
  5.8 0.8 copy-done.5
  6.6 112.9 %shard_map.103 = (f32[1,128]{1,0:T(1,128)S(1)}, f32[128,256]{1,0:T(8,128)S(1)}, bf16[128,256]{1,0:T(8,128)(2,1)S(1)}) custom-call(bf16[256,256]{1,0:T(8,128)(2,1)S(1)} %copy-done, bf16[256,256]{1,0:T(8,128)(2,1)S(1)} %copy-done.1, s32[1,128]{1,0:T(1,128)S(1)} %copy-done.6, s32[1]{0:T(128)S(6)} %copy.14.refs_3_, bf16[256,256]{1,0:T(8,128)(2,1)S(1)} %copy-done.2, ...), custom_call_target="tpu_custom_call" | custom-call | tf_op jit(solution)/shard_map/pallas_call | solution.py:364
  119.5 0.5 copy.15
  120.0 0.7 copy.16
  120.7 0.6 copy.17
Async XLA Ops:
  0.6 0.7 copy-start.6
  1.3 0.9 copy-start
  2.2 0.9 copy-start.1
  3.1 0.9 copy-start.2
  4.0 0.9 copy-start.3
  4.9 0.8 copy-start.4
  5.8 0.8 copy-start.5

commit v2 on v1

--- a/solution.py
+++ b/solution.py
@@ -32,14 +32,6 @@
 def unit_rows(v):
     length = jnp.sqrt(jnp.sum(v * v, axis=1, keepdims=True) + EPSILON)
     return v / length, length
-
-
-def split_rows(row):
-    wide = jnp.broadcast_to(row, (8, row.shape[1]))
-    high = wide.astype(BF16).astype(F32)
-    place = lax.broadcasted_iota(jnp.int32, wide.shape, 0)
-    picked = jnp.where(place == 0, high, jnp.where(place == 1, wide - high, 0.0))
-    return picked.astype(BF16)
 
 
 def column(row):
@@ -69,9 +61,9 @@
         "di_s": ((nv, rows, bot), BF16),
         "di_t": ((nv, rows, bot), BF16),
         "kf": ((nq, tok, 256), F32),
-        "kb": ((nq, tok, 256), BF16),
+        "db": ((nq, tok, 256), BF16),
         "ef": ((nq, tok, 256), F32),
-        "kl": ((nq, tok, 256), BF16),
+        "kl": ((nq, tok, 256), F32),
         "pb": ((ITERS, nv, nq, 256), F32),
         "pv": ((nq, 256), F32),
         "tz": ((ITERS - 1, NZ, 1, tok), F32),
@@ -81,6 +73,7 @@
         "fz": ((NZ, 2, tok), F32),
         "fc": ((NC, 2, tok), F32),
         "loss": ((tok, 128), F32),
+        "cols": ((2, tok, 128), F32),
         "lb": ((np_, own, 128), F32),
         "ug": ((NC, half, bot), F32),
         "ur": ((half, bot), F32),
@@ -102,10 +95,16 @@
         d["nx"], d["ny"], d["np"], d["nv"], d["own"], d["tok"], d["half"], d["nq"],
     )
     bot, rows, slots, patches, images = d["bot"], d["rows"], d["slots"], d["patches"], d["images"]
-    sh, th, idx, count, sb, tb, sp, tp, loss_out, proto_out, hidden_out = refs[:11]
+    given = refs[:8]
+    loss_out, proto_out, hidden_out = refs[8:11]
     vmem, sems = scratch_of(d)
     m = dict(zip(vmem, refs[11 : 11 + len(vmem)]))
-    send_sem, recv_sem = refs[11 + len(vmem) :]
+    held = refs[11 + len(vmem) : 19 + len(vmem)]
+    sh, th, idx, count, sb, tb, sp, tp = held
+    send_sem, recv_sem, load_sem = refs[19 + len(vmem) :]
+    loads = [pltpu.make_async_copy(given[i], held[i], load_sem.at[i]) for i in range(8)]
+    for i in (2, 1, 5, 0, 4, 7, 6, 3):
+        loads[i].start()
     number = {name: i for i, name in enumerate(sems)}
 
     dp, pr = lax.axis_index("dp"), lax.axis_index("proto")
@@ -163,11 +162,15 @@
     for device in peers:
         pl.semaphore_signal(barrier, inc=1, device_id=device, device_id_type=MESH)
 
+    for i in (2, 1, 5, 0, 4):
+        loads[i].wait()
     picked = twice(jnp.broadcast_to(idx[...].astype(F32), (128, slots)).T)
     patch = lax.broadcasted_iota(jnp.int32, (slots, patches), 1).astype(F32)
     one_hot = jnp.where(picked == patch, 1.0, 0.0).astype(BF16)
     m["zs_t"][...] = dot(dot(one_hot, th[...]).astype(BF16), tb[...]).reshape(np_, own, bot)
     m["zs_s"][...] = dot(dot(one_hot, sh[...]).astype(BF16), sb[...]).reshape(np_, own, bot)
+    for i in (7, 6, 3):
+        loads[i].wait()
     m["di_t"][v] = unit_rows(tp[...].astype(F32))[0].astype(BF16)
     m["di_s"][v] = unit_rows(sp[...].astype(F32))[0].astype(BF16)
     m["cnt"][z] = jnp.full((1, 128), count[0].astype(F32), F32)
@@ -179,7 +182,6 @@
         m["zr_" + name][pr] = m["zs_" + name][pr]
     to_z("cnt", m["cnt"].at[z], m["cnt"].at[z])
     to_v("di_t", m["di_t"].at[v], m["di_t"].at[v])
-    to_v("di_s", m["di_s"].at[v], m["di_s"].at[v])
 
     for name in ("t", "s"):
         arrived("zr_" + name, m["zr_" + name].at[pl.ds(0, np_ - 1)])
@@ -222,7 +224,6 @@
         logits = dot_last(units("t"), dirs("t", q))
         k_tile = live_col * jnp.exp2(logits * (LOG2E / TEACHER_TEMP))
         m["kf"][q] = k_tile
-        m["kb"][q] = k_tile.astype(BF16)
         m["pb"][0, v, pl.ds(q, 1), :] = jnp.sum(k_tile, axis=0, keepdims=True)
         return carry
 
@@ -233,28 +234,28 @@
         to_v("pb%d" % k, mine, mine)
 
     send_p(0)
-
-    whole_units("s")
-    arrived("di_s", m["di_s"].at[pl.ds(0, nv - 1)])
-    m["su_tr"][...] = units("s").astype(F32).T.astype(BF16)
-    ones = jnp.ones((8, 256), BF16)
 
     def student(q, total):
         logits = dot_last(units("s"), dirs("s", q))
         e_tile = jnp.exp2(logits * (LOG2E / STUDENT_TEMP))
         m["ef"][q] = e_tile
-        m["kl"][q] = (m["kf"][q] * logits).astype(BF16)
-        return total + dot_last(ones, e_tile.astype(BF16))
-
-    e_sum = lax.fori_loop(0, nq, student, jnp.zeros((8, tok), F32))
-    m["ez"][z] = e_sum[0:1]
-
-    def over_p(which):
-        def step(q, total):
-            return total + dot_last(split_rows(m["pv"][pl.ds(q, 1), :]), m[which][q])
-
-        total = lax.fori_loop(0, nq, step, jnp.zeros((8, tok), F32))
-        return total[0:1] + total[1:2]
+        m["kl"][q] = m["kf"][q] * logits
+        return total + e_tile[:, :128] + e_tile[:, 128:]
+
+    def over_p(which, out, place):
+        def block(b, carry):
+            at = pl.ds(pl.multiple_of(b * 128, 128), 128)
+            totals = [jnp.zeros((128, 128), F32) for _ in which]
+            for q in range(nq):
+                scale = m["pv"][q : q + 1, :]
+                for i, name in enumerate(which):
+                    part = m[name][q, at, :] * scale
+                    totals[i] += part[:, :128] + part[:, 128:]
+            for i, total in enumerate(totals):
+                out[place, i : i + 1, at] = jnp.sum(total.T, axis=0, keepdims=True)
+            return carry
+
+        lax.fori_loop(0, tok // 128, block, 0)
 
     def z_sum(name_z, name_c, z_buf, c_buf):
         arrived(name_z, z_buf.at[pl.ds(0, NZ - 1)])
@@ -265,67 +266,88 @@
         arrived(name_c, c_buf.at[0])
         return c_buf[0] + c_buf[1]
 
-    for k in range(ITERS):
+    for k in range(ITERS - 1):
         arrived("pb%d" % k, m["pb"].at[k, pl.ds(0, nv - 1)])
         m["pv"][...] = 1.0 / jnp.sum(m["pb"][k], axis=0)
-        if k == ITERS - 1:
-            break
         z_buf, c_buf = m["tz"].at[k], m["tc"].at[k]
-        z_buf[z] = over_p("kb")
+        over_p(["kf"], z_buf, z)
         to_z("tz%d" % k, z_buf.at[z], z_buf.at[z])
+        part = m["di_s"].at[v, pl.ds(k * (rows // 2), rows // 2)]
+        to_v("di_s", part, part)
         if k == 0:
-            to_z("ez", m["ez"].at[z], m["ez"].at[z])
+            whole_units("s")
+            m["su_tr"][...] = units("s").astype(F32).T.astype(BF16)
         z_sum("tz%d" % k, "tc%d" % k, z_buf, c_buf)
         total = c_sum("tc%d" % k, c_buf)
-        t_rows = split_rows(1.0 / jnp.where(live > 0, total, 1.0))
+        t_col = twice(column(1.0 / jnp.where(live > 0, total, 1.0)))
 
         def over_t(q, carry):
-            part = dot(t_rows, m["kb"][q])
-            m["pb"][k + 1, v, pl.ds(q, 1), :] = part[0:1] + part[1:2]
+            m["pb"][k + 1, v, pl.ds(q, 1), :] = jnp.sum(m["kf"][q] * t_col, axis=0, keepdims=True)
             return carry
 
         lax.fori_loop(0, nq, over_t, 0)
         send_p(k + 1)
-        if k == 0:
-            z_sum("ez", "ec", m["ez"], m["ec"])
-
-    m["fz"][z] = jnp.concatenate([over_p("kb"), over_p("kl")], axis=0)
+    arrived("di_s", m["di_s"].at[pl.ds(0, nv - 1)])
+    e_sum = lax.fori_loop(0, nq, student, jnp.zeros((tok, 128), F32))
+    m["ez"][z] = jnp.sum(e_sum.T, axis=0, keepdims=True)
+    to_z("ez", m["ez"].at[z], m["ez"].at[z])
+    arrived("pb2", m["pb"].at[2, pl.ds(0, nv - 1)])
+    m["pv"][...] = 1.0 / jnp.sum(m["pb"][2], axis=0)
+    over_p(["kf", "kl"], m["fz"], z)
     to_z("fz", m["fz"].at[z], m["fz"].at[z])
+    z_sum("ez", "ec", m["ez"], m["ec"])
     total_z = c_sum("ec", m["ec"])
     weight = live * (GRAD_SCALE / STUDENT_TEMP) / (counts * images)
-    e_col = twice(column(weight / total_z))
+    m["cols"][0] = column(weight / total_z)
     z_sum("fz", "fc", m["fz"], m["fc"])
     last = c_sum("fc", m["fc"])
     t_row = 1.0 / jnp.where(live > 0, last[0:1], 1.0)
+    m["cols"][1] = column(weight * t_row)
     total_ts = last[1:2] * t_row
     m["loss"][...] = column(live * (jnp.log(total_z) - total_ts / STUDENT_TEMP))
-    k_col = twice(column(weight * t_row))
 
     m["lb"][pr] = m["loss"][pl.ds(pl.multiple_of((c * NZ + z) * own, own), own), :]
     for other in pr_peers:
         push("lb", m["lb"].at[pr], m["lb"].at[pr], at_pr(other))
 
-    m["ug"][...] = jnp.zeros((NC, half, bot), F32)
-
-    def grads(q, carry):
-        targets = k_col * (m["kf"][q] * m["pv"][pl.ds(q, 1), :])
-        d_tile = (e_col * m["ef"][q] - targets).astype(BF16)
-        m["ug"][...] += dot(d_tile, dirs("s", q)).reshape(NC, half, bot)
-        raw = dot(m["su_tr"][...], d_tile).astype(BF16)
-        m["rs"][2 * q] = raw[:, :rows]
-        m["rs"][2 * q + 1] = raw[:, rows:]
-        return carry
-
-    lax.fori_loop(0, nq, grads, 0)
+    def unit_grads(side):
+        at = pl.ds(pl.multiple_of(side * half, half), half)
+        m["ug"][side] = jnp.zeros((half, bot), F32)
+
+        def step(q, carry):
+            e_col, k_col = twice(m["cols"][0, at, :]), twice(m["cols"][1, at, :])
+            targets = k_col * (m["kf"][q, at, :] * m["pv"][pl.ds(q, 1), :])
+            d_tile = (e_col * m["ef"][q, at, :] - targets).astype(BF16)
+            m["db"][q, at, :] = d_tile
+            m["ug"][side] += dot(d_tile, dirs("s", q))
+            return carry
+
+        lax.fori_loop(0, nq, step, 0)
+
+    unit_grads(1 - c)
     push("ur", m["ug"].at[1 - c], m["ur"], sibling)
-    for other in v_peers:
-        push("rr", m["rs"].at[other[0] * ny + other[1]], m["rr"].at[v], at_v(other))
-    m["rr"][v] = m["rs"][v]
+    unit_grads(c)
     arrived("ur", m["ur"])
     m["us"][...] = (m["ug"][c] + m["ur"][...]).astype(BF16).reshape(NZ, own, bot)
     for other in z_peers:
         push("uz", m["us"].at[other], m["uz"].at[z], at_z(other))
     m["uz"][z] = m["us"][z]
+
+    def raw_grads(step, carry):
+        q = lax.rem(step + v // 2, nq)
+        raw = dot(m["su_tr"][...], m["db"][q]).astype(BF16)
+        for j in range(256 // rows):
+            other = 2 * q + j
+            m["rs"][other] = raw[:, j * rows : (j + 1) * rows]
+
+            @pl.when(other != v)
+            def _():
+                push("rr", m["rs"].at[other], m["rr"].at[v], at_v((other // ny, lax.rem(other, ny))))
+
+        return carry
+
+    lax.fori_loop(0, nq, raw_grads, 0)
+    m["rr"][v] = m["rs"][v]
     arrived("uz", m["uz"].at[pl.ds(0, NZ - 1)])
     unit_grad = jnp.sum(m["uz"][...].astype(F32), axis=0)
     own_z, length = m["zown"][...], m["zlen"][:, 0:1]
@@ -361,6 +383,9 @@
     d["patches"] = sh.shape[0]
     vmem, sems = scratch_of(d)
     vm = pl.BlockSpec(memory_space=pltpu.VMEM)
+    args = (sh, th, idx, count, sb, tb, sp, tp)
+    held = [pltpu.VMEM(a.shape, a.dtype) for a in args]
+    held[3] = pltpu.SMEM(count.shape, count.dtype)
     loss, proto_grad, hidden_grad = pl.pallas_call(
         functools.partial(kernel, d),
         out_shape=(
@@ -368,14 +393,15 @@
             jax.ShapeDtypeStruct(sp.shape, F32),
             jax.ShapeDtypeStruct((d["slots"], sb.shape[0]), BF16),
         ),
-        in_specs=[vm, vm, vm, pl.BlockSpec(memory_space=pltpu.SMEM), vm, vm, vm, vm],
+        in_specs=[pl.BlockSpec(memory_space=pltpu.HBM)] * 8,
         out_specs=(vm, vm, vm),
         scratch_shapes=[pltpu.VMEM(shape, dtype) for shape, dtype in vmem.values()]
-        + [pltpu.SemaphoreType.DMA((len(sems),)), pltpu.SemaphoreType.DMA((len(sems),))],
+        + held
+        + [pltpu.SemaphoreType.DMA((n,)) for n in (len(sems), len(sems), len(args))],
         compiler_params=pltpu.CompilerParams(
-            collective_id=0, has_side_effects=True, vmem_limit_bytes=48 * 2**20
+            collective_id=0, has_side_effects=True, vmem_limit_bytes=64 * 2**20
         ),
-    )(sh, th, idx, count, sb, tb, sp, tp)
+    )(*args)
     return loss.reshape(-1), proto_grad, hidden_grad
 
 

time: 122 us -> 114 us (0.934)
  Pallas kernels: 113 us -> 108 us
  local copies, waits for them, and re-layouts: 7.09 us -> 3.37 us
    pallas_call x1, Pallas kernels: 113 us -> 108 us  [body(): pl.pallas_call(functools.partial(kernel, d), out_shape=(jax.ShapeDtypeStr...]
    unnamed x17 -> x7, local copies, waits for them, and re-layouts: 7.09 us -> 3.37 us
where the time goes in v2:
time: 114 us; the launch traced here: 113 us
  Pallas kernels  108 us (95%)
  local copies, waits for them, and re-layouts  3.37 us (3%)
  between operations  1.3 us (1%)
    pallas_call x1, Pallas kernels, body(): pl.pallas_call(functools.partial(kernel, d), out_shape=(jax.ShapeDtypeStr...  108 us
    unnamed x7, local copies, waits for them, and re-layouts  3.37 us

profile of v2, /device:TPU:1, one launch (start us, length us, event | category | flops | bytes accessed | tf_op | source)
XLA Modules:
  0.0 112.7 jit_solution(1496485598665467448)
XLA Ops:
  1.3 108.1 %shard_map.103 = (f32[1,128]{1,0:T(1,128)}, f32[128,256]{1,0:T(8,128)}, bf16[128,256]{1,0:T(8,128)(2,1)}) custom-call(bf16[256,256]{1,0:T(8,128)(2,1)} %refs_0_.1, bf16[256,256]{1,0:T(8,128)(2,1)} %refs_1_.1, s32[1,128]{1,0:T(1,128)} %refs_2_.1, s32[1]{0:T(128)S(6)} %copy.14.refs_3_, bf16[256,256]{1,0:T(8,128)(2,1)} %refs_4_.1, bf16[256,256]{1,0:T(8,128)(2,1)} %refs_5_.1, ...), custom_call_target="tpu_custom_call" | custom-call | tf_op jit(solution)/shard_map/pallas_call | solution.py:389
  109.4 0.0 copy-start.1
  109.4 0.6 copy-done.1
  110.0 0.5 copy.15
  110.5 0.0 copy-start
  110.5 1.6 %copy.16 = f32[128,256]{1,0:T(8,128)} copy(f32[128,256]{1,0:T(8,128)} %get-tuple-element.13) | data formatting | bytes 262144
  112.1 0.0 copy-done
  112.1 0.6 copy.17
Async XLA Ops:
  109.4 0.6 copy-start.1
  110.5 1.6 %copy-start = (bf16[128,256]{1,0:T(8,128)(2,1)S(1)}, bf16[128,256]{1,0:T(8,128)(2,1)}, u32[]{:S(2)}) copy-start(bf16[128,256]{1,0:T(8,128)(2,1)} %get-tuple-element.14) | copy-start | bytes 196612

commit v3 on v2

--- a/solution.py
+++ b/solution.py
@@ -61,7 +61,7 @@
         "di_s": ((nv, rows, bot), BF16),
         "di_t": ((nv, rows, bot), BF16),
         "kf": ((nq, tok, 256), F32),
-        "db": ((nq, tok, 256), BF16),
+        "db": ((tok, nq * 256), BF16),
         "ef": ((nq, tok, 256), F32),
         "kl": ((nq, tok, 256), F32),
         "pb": ((ITERS, nv, nq, 256), F32),
@@ -162,29 +162,34 @@
     for device in peers:
         pl.semaphore_signal(barrier, inc=1, device_id=device, device_id_type=MESH)
 
-    for i in (2, 1, 5, 0, 4):
+    for i in (2, 1, 5):
         loads[i].wait()
     picked = twice(jnp.broadcast_to(idx[...].astype(F32), (128, slots)).T)
     patch = lax.broadcasted_iota(jnp.int32, (slots, patches), 1).astype(F32)
     one_hot = jnp.where(picked == patch, 1.0, 0.0).astype(BF16)
-    m["zs_t"][...] = dot(dot(one_hot, th[...]).astype(BF16), tb[...]).reshape(np_, own, bot)
-    m["zs_s"][...] = dot(dot(one_hot, sh[...]).astype(BF16), sb[...]).reshape(np_, own, bot)
-    for i in (7, 6, 3):
+
+    def send_partial(name, hidden, bottle):
+        parts = dot(dot(one_hot, hidden[...]).astype(BF16), bottle[...])
+        m["zs_" + name][...] = parts.reshape(np_, own, bot)
+        if name == "t":
+            pl.semaphore_wait(barrier, len(peers))
+        for other in pr_peers:
+            push("zr_" + name, m["zs_" + name].at[other], m["zr_" + name].at[pr], at_pr(other))
+        m["zr_" + name][pr] = m["zs_" + name][pr]
+
+    send_partial("t", th, tb)
+    for i in (0, 4, 7, 6, 3):
         loads[i].wait()
+    send_partial("s", sh, sb)
     m["di_t"][v] = unit_rows(tp[...].astype(F32))[0].astype(BF16)
     m["di_s"][v] = unit_rows(sp[...].astype(F32))[0].astype(BF16)
     m["cnt"][z] = jnp.full((1, 128), count[0].astype(F32), F32)
-
-    pl.semaphore_wait(barrier, len(peers))
-    for name in ("t", "s"):
-        for other in pr_peers:
-            push("zr_" + name, m["zs_" + name].at[other], m["zr_" + name].at[pr], at_pr(other))
-        m["zr_" + name][pr] = m["zs_" + name][pr]
     to_z("cnt", m["cnt"].at[z], m["cnt"].at[z])
-    to_v("di_t", m["di_t"].at[v], m["di_t"].at[v])
 
     for name in ("t", "s"):
         arrived("zr_" + name, m["zr_" + name].at[pl.ds(0, np_ - 1)])
+        if name == "t":
+            to_v("di_t", m["di_t"].at[v], m["di_t"].at[v])
         own_z = jnp.sum(m["zr_" + name][...], axis=0)
         unit, length = unit_rows(own_z)
         m["un_" + name][c, z] = unit.astype(BF16)
@@ -227,7 +232,7 @@
         m["pb"][0, v, pl.ds(q, 1), :] = jnp.sum(k_tile, axis=0, keepdims=True)
         return carry
 
-    lax.fori_loop(0, nq, teacher, 0)
+    lax.fori_loop(0, nq, teacher, 0, unroll=2)
 
     def send_p(k):
         mine = m["pb"].at[k, v]
@@ -310,19 +315,33 @@
     for other in pr_peers:
         push("lb", m["lb"].at[pr], m["lb"].at[pr], at_pr(other))
 
+    e_col, k_col = twice(m["cols"][0]), twice(m["cols"][1])
+
+    def block_grads(q):
+        targets = k_col * (m["kf"][q] * m["pv"][pl.ds(q, 1), :])
+        d_tile = (e_col * m["ef"][q] - targets).astype(BF16)
+        m["db"][:, pl.ds(pl.multiple_of(q * 256, 256), 256)] = d_tile
+        raw = dot(m["su_tr"][...], d_tile).astype(BF16)
+        m["rs"][2 * q] = raw[:, :rows]
+        m["rs"][2 * q + 1] = raw[:, rows:]
+
+    def send_raw(other):
+        push("rr", m["rs"].at[other], m["rr"].at[v], at_v((other // ny, lax.rem(other, ny))))
+
+    for step in range(1, nq + 1):
+        q = lax.rem(step + v // 2, nq)
+        block_grads(q)
+        if step < nq:
+            send_raw(2 * q)
+            send_raw(2 * q + 1)
+    send_raw(v + 1 - 2 * lax.rem(v, 2))
+    m["rr"][v] = m["rs"][v]
+
+    all_dirs = m["di_s"][...].reshape(nq * 256, bot)
+
     def unit_grads(side):
         at = pl.ds(pl.multiple_of(side * half, half), half)
-        m["ug"][side] = jnp.zeros((half, bot), F32)
-
-        def step(q, carry):
-            e_col, k_col = twice(m["cols"][0, at, :]), twice(m["cols"][1, at, :])
-            targets = k_col * (m["kf"][q, at, :] * m["pv"][pl.ds(q, 1), :])
-            d_tile = (e_col * m["ef"][q, at, :] - targets).astype(BF16)
-            m["db"][q, at, :] = d_tile
-            m["ug"][side] += dot(d_tile, dirs("s", q))
-            return carry
-
-        lax.fori_loop(0, nq, step, 0)
+        m["ug"][side] = dot(m["db"][at, :], all_dirs)
 
     unit_grads(1 - c)
     push("ur", m["ug"].at[1 - c], m["ur"], sibling)
@@ -332,22 +351,6 @@
     for other in z_peers:
         push("uz", m["us"].at[other], m["uz"].at[z], at_z(other))
     m["uz"][z] = m["us"][z]
-
-    def raw_grads(step, carry):
-        q = lax.rem(step + v // 2, nq)
-        raw = dot(m["su_tr"][...], m["db"][q]).astype(BF16)
-        for j in range(256 // rows):
-            other = 2 * q + j
-            m["rs"][other] = raw[:, j * rows : (j + 1) * rows]
-
-            @pl.when(other != v)
-            def _():
-                push("rr", m["rs"].at[other], m["rr"].at[v], at_v((other // ny, lax.rem(other, ny))))
-
-        return carry
-
-    lax.fori_loop(0, nq, raw_grads, 0)
-    m["rr"][v] = m["rs"][v]
     arrived("uz", m["uz"].at[pl.ds(0, NZ - 1)])
     unit_grad = jnp.sum(m["uz"][...].astype(F32), axis=0)
     own_z, length = m["zown"][...], m["zlen"][:, 0:1]
@@ -369,6 +372,19 @@
 
     for name, like in sent:
         pltpu.make_async_copy(like, like, send_sem.at[number[name]]).wait()
+
+
+def hand_over(*refs):
+    sem = refs[9]
+    loads = [pltpu.make_async_copy(refs[i], refs[i + 6], sem.at[i]) for i in range(3)]
+    stores = [pltpu.make_async_copy(refs[i + 6], refs[i + 3], sem.at[i + 3]) for i in range(3)]
+    for load in loads:
+        load.start()
+    for load, store in zip(loads, stores):
+        load.wait()
+        store.start()
+    for store in stores:
+        store.wait()
 
 
 def body(sh, th, idx, count, sb, tb, sp, tp):
@@ -386,7 +402,7 @@
     args = (sh, th, idx, count, sb, tb, sp, tp)
     held = [pltpu.VMEM(a.shape, a.dtype) for a in args]
     held[3] = pltpu.SMEM(count.shape, count.dtype)
-    loss, proto_grad, hidden_grad = pl.pallas_call(
+    results = pl.pallas_call(
         functools.partial(kernel, d),
         out_shape=(
             jax.ShapeDtypeStruct((1, d["slots"]), F32),
@@ -402,6 +418,14 @@
             collective_id=0, has_side_effects=True, vmem_limit_bytes=64 * 2**20
         ),
     )(*args)
+    hbm = pl.BlockSpec(memory_space=pltpu.HBM)
+    loss, proto_grad, hidden_grad = pl.pallas_call(
+        hand_over,
+        out_shape=tuple(jax.ShapeDtypeStruct(r.shape, r.dtype) for r in results),
+        in_specs=[hbm] * 3,
+        out_specs=(hbm,) * 3,
+        scratch_shapes=[pltpu.VMEM(r.shape, r.dtype) for r in results] + [pltpu.SemaphoreType.DMA((6,))],
+    )(*results)
     return loss.reshape(-1), proto_grad, hidden_grad
 
 

time: 114 us -> 105 us (0.921)
  Pallas kernels: 108 us -> 103 us
  local copies, waits for them, and re-layouts: 3.37 us -> 0 us
    pallas_call x1, Pallas kernels: 108 us -> 101 us  [body(): pl.pallas_call(functools.partial(kernel, d), out_shape=(jax.ShapeDtypeStr...]
    unnamed x7 -> x0, local copies, waits for them, and re-layouts: 3.37 us -> none
    pallas_call x0 -> x1, Pallas kernels: none -> 1.63 us  [body(): pl.pallas_call(hand_over, out_shape=tuple((jax.ShapeDtypeStruct(r.shape,...]
where the time goes in v3:
time: 105 us; the launch traced here: 104 us
  Pallas kernels  103 us (98%)
  between operations  1.29 us (1%)
    pallas_call x1, Pallas kernels, body(): pl.pallas_call(functools.partial(kernel, d), out_shape=(jax.ShapeDtypeStr...  101 us

profile of v3, /device:TPU:1, one launch (start us, length us, event | category | flops | bytes accessed | tf_op | source)
XLA Modules:
  0.0 104.4 jit_solution(6887314371282052788)
XLA Ops:
  1.3 101.5 %shard_map.103 = (f32[1,128]{1,0:T(1,128)}, f32[128,256]{1,0:T(8,128)}, bf16[128,256]{1,0:T(8,128)(2,1)}) custom-call(bf16[256,256]{1,0:T(8,128)(2,1)} %refs_0_.1, bf16[256,256]{1,0:T(8,128)(2,1)} %refs_1_.1, s32[1,128]{1,0:T(1,128)} %refs_2_.1, s32[1]{0:T(128)S(6)} %copy.11.refs_3_, bf16[256,256]{1,0:T(8,128)(2,1)} %refs_4_.1, bf16[256,256]{1,0:T(8,128)(2,1)} %refs_5_.1, ...), custom_call_target="tpu_custom_call" | custom-call | tf_op jit(solution)/shard_map/pallas_call | solution.py:405
  102.8 1.6 %shard_map.104 = (f32[1,128]{1,0:T(1,128)}, f32[128,256]{1,0:T(8,128)}, bf16[128,256]{1,0:T(8,128)(2,1)}) custom-call(f32[1,128]{1,0:T(1,128)} %get-tuple-element.9.refs_0_, f32[128,256]{1,0:T(8,128)} %get-tuple-element.10.refs_1_, bf16[128,256]{1,0:T(8,128)(2,1)} %get-tuple-element.11.refs_2_), custom_call_target="tpu_custom_call" | custom-call | tf_op jit(solution)/shard_map/pallas_call | solution.py:422

commit v4 on v3

--- a/solution.py
+++ b/solution.py
@@ -61,31 +61,35 @@
         "di_s": ((nv, rows, bot), BF16),
         "di_t": ((nv, rows, bot), BF16),
         "kf": ((nq, tok, 256), F32),
-        "db": ((tok, nq * 256), BF16),
+        "eb": ((tok, nq * 256), BF16),
+        "kb": ((tok, nq * 256), BF16),
         "ef": ((nq, tok, 256), F32),
         "kl": ((nq, tok, 256), F32),
-        "pb": ((ITERS, nv, nq, 256), F32),
+        "pb": ((ITERS, nv, 2 * nq, 128), BF16),
+        "pp": ((nq, 256), F32),
         "pv": ((nq, 256), F32),
         "tz": ((ITERS - 1, NZ, 1, tok), F32),
         "tc": ((ITERS - 1, NC, 1, tok), F32),
         "ez": ((NZ, 1, tok), F32),
         "ec": ((NC, 1, tok), F32),
-        "fz": ((NZ, 2, tok), F32),
-        "fc": ((NC, 2, tok), F32),
+        "fz": ((NZ, 1, tok), F32),
+        "fc": ((NC, 1, tok), F32),
+        "sz": ((NZ, 1, tok), F32),
+        "sc": ((NC, 1, tok), F32),
         "loss": ((tok, 128), F32),
         "cols": ((2, tok, 128), F32),
         "lb": ((np_, own, 128), F32),
-        "ug": ((NC, half, bot), F32),
-        "ur": ((half, bot), F32),
-        "us": ((NZ, own, bot), BF16),
-        "uz": ((NZ, own, bot), BF16),
+        "ug": ((NC, 2, half, bot), F32),
+        "ur": ((2, half, bot), F32),
+        "us": ((NZ, 2, own, bot), BF16),
+        "uz": ((NZ, 2, own, bot), BF16),
         "rs": ((nv, bot, rows), BF16),
         "rr": ((nv, bot, rows), BF16),
         "bg": ((np_, own, bot), BF16),
     }
     sems = [
         "zr_s", "zr_t", "cnt", "un_s", "un_t", "uc_s", "uc_t", "di_s", "di_t", "pb0", "pb1", "pb2",
-        "tz0", "tz1", "tc0", "tc1", "ez", "ec", "fz", "fc", "lb", "ur", "uz", "rr", "bg",
+        "tz0", "tz1", "tc0", "tc1", "ez", "ec", "fz", "fc", "sz", "sc", "lb", "ur", "uz", "rr", "bg",
     ]
     return vmem, sems
 
@@ -114,11 +118,11 @@
     z_order = sorted(range(1, NZ), key=lambda k: -min(k, NZ - k))
     z_peers = [lax.rem(z + k, NZ) for k in z_order]
     pr_peers = [lax.rem(pr + k, np_) for k in range(1, np_)]
-    v_peers = []
-    for k in range(nx):
-        for j in range(ny):
-            if k or j:
-                v_peers.append((lax.rem(x + k, nx), lax.rem(y + j, ny)))
+    v_order = sorted(
+        ((k, j) for k in range(nx) for j in range(ny) if k or j),
+        key=lambda kj: -(min(kj[0], nx - kj[0]) + min(kj[1], ny - kj[1])),
+    )
+    v_peers = [(lax.rem(x + k, nx), lax.rem(y + j, ny)) for k, j in v_order]
 
     def at_z(other):
         return (x * NZ + other, pr)
@@ -229,12 +233,14 @@
         logits = dot_last(units("t"), dirs("t", q))
         k_tile = live_col * jnp.exp2(logits * (LOG2E / TEACHER_TEMP))
         m["kf"][q] = k_tile
-        m["pb"][0, v, pl.ds(q, 1), :] = jnp.sum(k_tile, axis=0, keepdims=True)
+        m["pp"][pl.ds(q, 1), :] = jnp.sum(k_tile, axis=0, keepdims=True)
         return carry
 
-    lax.fori_loop(0, nq, teacher, 0, unroll=2)
+    lax.fori_loop(0, nq, teacher, 0, unroll=4 if nq % 4 == 0 else 1)
 
     def send_p(k):
+        part = jnp.concatenate([m["pp"][:, :128], m["pp"][:, 128:]], axis=0)
+        m["pb"][k, v] = part.astype(BF16)
         mine = m["pb"].at[k, v]
         to_v("pb%d" % k, mine, mine)
 
@@ -244,20 +250,23 @@
         logits = dot_last(units("s"), dirs("s", q))
         e_tile = jnp.exp2(logits * (LOG2E / STUDENT_TEMP))
         m["ef"][q] = e_tile
+        m["eb"][:, pl.ds(pl.multiple_of(q * 256, 256), 256)] = e_tile.astype(BF16)
         m["kl"][q] = m["kf"][q] * logits
         return total + e_tile[:, :128] + e_tile[:, 128:]
 
-    def over_p(which, out, place):
+    def take_p(k):
+        arrived("pb%d" % k, m["pb"].at[k, pl.ds(0, nv - 1)])
+        total = jnp.sum(m["pb"][k].astype(F32), axis=0)
+        m["pv"][...] = 1.0 / jnp.concatenate([total[:nq], total[nq:]], axis=1)
+
+    def over_p(name, out):
         def block(b, carry):
             at = pl.ds(pl.multiple_of(b * 128, 128), 128)
-            totals = [jnp.zeros((128, 128), F32) for _ in which]
+            total = jnp.zeros((128, 128), F32)
             for q in range(nq):
-                scale = m["pv"][q : q + 1, :]
-                for i, name in enumerate(which):
-                    part = m[name][q, at, :] * scale
-                    totals[i] += part[:, :128] + part[:, 128:]
-            for i, total in enumerate(totals):
-                out[place, i : i + 1, at] = jnp.sum(total.T, axis=0, keepdims=True)
+                part = m[name][q, at, :] * m["pv"][q : q + 1, :]
+                total += part[:, :128] + part[:, 128:]
+            out[z, :, at] = jnp.sum(total.T, axis=0, keepdims=True)
             return carry
 
         lax.fori_loop(0, tok // 128, block, 0)
@@ -272,10 +281,9 @@
         return c_buf[0] + c_buf[1]
 
     for k in range(ITERS - 1):
-        arrived("pb%d" % k, m["pb"].at[k, pl.ds(0, nv - 1)])
-        m["pv"][...] = 1.0 / jnp.sum(m["pb"][k], axis=0)
+        take_p(k)
         z_buf, c_buf = m["tz"].at[k], m["tc"].at[k]
-        over_p(["kf"], z_buf, z)
+        over_p("kf", z_buf)
         to_z("tz%d" % k, z_buf.at[z], z_buf.at[z])
         part = m["di_s"].at[v, pl.ds(k * (rows // 2), rows // 2)]
         to_v("di_s", part, part)
@@ -287,7 +295,7 @@
         t_col = twice(column(1.0 / jnp.where(live > 0, total, 1.0)))
 
         def over_t(q, carry):
-            m["pb"][k + 1, v, pl.ds(q, 1), :] = jnp.sum(m["kf"][q] * t_col, axis=0, keepdims=True)
+            m["pp"][pl.ds(q, 1), :] = jnp.sum(m["kf"][q] * t_col, axis=0, keepdims=True)
             return carry
 
         lax.fori_loop(0, nq, over_t, 0)
@@ -296,31 +304,49 @@
     e_sum = lax.fori_loop(0, nq, student, jnp.zeros((tok, 128), F32))
     m["ez"][z] = jnp.sum(e_sum.T, axis=0, keepdims=True)
     to_z("ez", m["ez"].at[z], m["ez"].at[z])
-    arrived("pb2", m["pb"].at[2, pl.ds(0, nv - 1)])
-    m["pv"][...] = 1.0 / jnp.sum(m["pb"][2], axis=0)
-    over_p(["kf", "kl"], m["fz"], z)
+    take_p(2)
+    over_p("kf", m["fz"])
     to_z("fz", m["fz"].at[z], m["fz"].at[z])
+    over_p("kl", m["sz"])
+    to_z("sz", m["sz"].at[z], m["sz"].at[z])
+
+    all_dirs = m["di_s"][...].reshape(nq * 256, bot)
+
+    def scaled(q, carry):
+        part = m["kf"][q] * m["pv"][pl.ds(q, 1), :]
+        m["kb"][:, pl.ds(pl.multiple_of(q * 256, 256), 256)] = part.astype(BF16)
+        return carry
+
+    lax.fori_loop(0, nq, scaled, 0)
+
+    def unit_terms(side):
+        at = pl.ds(pl.multiple_of(side * half, half), half)
+        m["ug"][side, 0] = dot(m["eb"][at, :], all_dirs)
+        m["ug"][side, 1] = dot(m["kb"][at, :], all_dirs)
+
+    unit_terms(1 - c)
+    push("ur", m["ug"].at[1 - c], m["ur"], sibling)
+    unit_terms(c)
     z_sum("ez", "ec", m["ez"], m["ec"])
+    arrived("ur", m["ur"])
+    for i in range(2):
+        m["us"][:, i] = (m["ug"][c, i] + m["ur"][i]).astype(BF16).reshape(NZ, own, bot)
+    for other in z_peers:
+        push("uz", m["us"].at[other], m["uz"].at[z], at_z(other))
+    m["uz"][z] = m["us"][z]
+
     total_z = c_sum("ec", m["ec"])
     weight = live * (GRAD_SCALE / STUDENT_TEMP) / (counts * images)
     m["cols"][0] = column(weight / total_z)
     z_sum("fz", "fc", m["fz"], m["fc"])
-    last = c_sum("fc", m["fc"])
-    t_row = 1.0 / jnp.where(live > 0, last[0:1], 1.0)
+    t_row = 1.0 / jnp.where(live > 0, c_sum("fc", m["fc"]), 1.0)
     m["cols"][1] = column(weight * t_row)
-    total_ts = last[1:2] * t_row
-    m["loss"][...] = column(live * (jnp.log(total_z) - total_ts / STUDENT_TEMP))
-
-    m["lb"][pr] = m["loss"][pl.ds(pl.multiple_of((c * NZ + z) * own, own), own), :]
-    for other in pr_peers:
-        push("lb", m["lb"].at[pr], m["lb"].at[pr], at_pr(other))
 
     e_col, k_col = twice(m["cols"][0]), twice(m["cols"][1])
 
     def block_grads(q):
         targets = k_col * (m["kf"][q] * m["pv"][pl.ds(q, 1), :])
         d_tile = (e_col * m["ef"][q] - targets).astype(BF16)
-        m["db"][:, pl.ds(pl.multiple_of(q * 256, 256), 256)] = d_tile
         raw = dot(m["su_tr"][...], d_tile).astype(BF16)
         m["rs"][2 * q] = raw[:, :rows]
         m["rs"][2 * q + 1] = raw[:, rows:]
@@ -328,7 +354,7 @@
     def send_raw(other):
         push("rr", m["rs"].at[other], m["rr"].at[v], at_v((other // ny, lax.rem(other, ny))))
 
-    for step in range(1, nq + 1):
+    for step in [*range(nq - 1, 0, -1), nq]:
         q = lax.rem(step + v // 2, nq)
         block_grads(q)
         if step < nq:
@@ -337,38 +363,33 @@
     send_raw(v + 1 - 2 * lax.rem(v, 2))
     m["rr"][v] = m["rs"][v]
 
-    all_dirs = m["di_s"][...].reshape(nq * 256, bot)
-
-    def unit_grads(side):
-        at = pl.ds(pl.multiple_of(side * half, half), half)
-        m["ug"][side] = dot(m["db"][at, :], all_dirs)
-
-    unit_grads(1 - c)
-    push("ur", m["ug"].at[1 - c], m["ur"], sibling)
-    unit_grads(c)
-    arrived("ur", m["ur"])
-    m["us"][...] = (m["ug"][c] + m["ur"][...]).astype(BF16).reshape(NZ, own, bot)
-    for other in z_peers:
-        push("uz", m["us"].at[other], m["uz"].at[z], at_z(other))
-    m["uz"][z] = m["us"][z]
+    z_sum("sz", "sc", m["sz"], m["sc"])
+    total_ts = c_sum("sc", m["sc"]) * t_row
+    m["loss"][...] = column(live * (jnp.log(total_z) - total_ts / STUDENT_TEMP))
+    mine = pl.ds(pl.multiple_of((c * NZ + z) * own, own), own)
+    m["lb"][pr] = m["loss"][mine, :]
+    for other in pr_peers:
+        push("lb", m["lb"].at[pr], m["lb"].at[pr], at_pr(other))
+
     arrived("uz", m["uz"].at[pl.ds(0, NZ - 1)])
-    unit_grad = jnp.sum(m["uz"][...].astype(F32), axis=0)
+    terms = jnp.sum(m["uz"][...].astype(F32), axis=0)
+    unit_grad = m["cols"][0, mine, 0:1] * terms[0] - m["cols"][1, mine, 0:1] * terms[1]
     own_z, length = m["zown"][...], m["zlen"][:, 0:1]
     along = jnp.sum(own_z * unit_grad, axis=1, keepdims=True)
     m["bg"][pr] = (unit_grad / length - own_z * along / length**3).astype(BF16)
     for other in pr_peers:
         push("bg", m["bg"].at[pr], m["bg"].at[pr], at_pr(other))
 
+    arrived("lb", m["lb"].at[pl.ds(0, np_ - 1)])
+    loss_out[...] = m["lb"][...].reshape(slots, 128).T[0:1]
+    arrived("bg", m["bg"].at[pl.ds(0, np_ - 1)])
+    hidden_out[...] = dot_last(m["bg"][...].reshape(slots, bot), sb[...]).astype(BF16)
+
     arrived("rr", m["rr"].at[pl.ds(0, nv - 1)])
     raw_grad = jnp.sum(m["rr"][...].astype(F32), axis=0).T
     own_raw = sp[...].astype(F32)
     norm = unit_rows(own_raw)[1]
     proto_out[...] = raw_grad / norm - own_raw * jnp.sum(own_raw * raw_grad, axis=1, keepdims=True) / norm**3
-
-    arrived("lb", m["lb"].at[pl.ds(0, np_ - 1)])
-    loss_out[...] = m["lb"][...].reshape(slots, 128).T[0:1]
-    arrived("bg", m["bg"].at[pl.ds(0, np_ - 1)])
-    hidden_out[...] = dot_last(m["bg"][...].reshape(slots, bot), sb[...]).astype(BF16)
 
     for name, like in sent:
         pltpu.make_async_copy(like, like, send_sem.at[number[name]]).wait()

time: 105 us -> 101 us (0.962)
  Pallas kernels: 103 us -> 99 us
    pallas_call x1, Pallas kernels: 101 us -> 97.4 us  [body(): pl.pallas_call(functools.partial(kernel, d), out_shape=(jax.ShapeDtypeStr...]
where the time goes in v4:
time: 101 us; the launch traced here: 100 us
  Pallas kernels  99 us (98%)
  between operations  1.29 us (1%)
    pallas_call x1, Pallas kernels, body(): pl.pallas_call(functools.partial(kernel, d), out_shape=(jax.ShapeDtypeStr...  97.4 us

profile of v4, /device:TPU:1, one launch (start us, length us, event | category | flops | bytes accessed | tf_op | source)
XLA Modules:
  0.0 100.3 jit_solution(14589428906209637277)
XLA Ops:
  1.3 97.4 %shard_map.103 = (f32[1,128]{1,0:T(1,128)}, f32[128,256]{1,0:T(8,128)}, bf16[128,256]{1,0:T(8,128)(2,1)}) custom-call(bf16[256,256]{1,0:T(8,128)(2,1)} %refs_0_.1, bf16[256,256]{1,0:T(8,128)(2,1)} %refs_1_.1, s32[1,128]{1,0:T(1,128)} %refs_2_.1, s32[1]{0:T(128)S(6)} %copy.11.refs_3_, bf16[256,256]{1,0:T(8,128)(2,1)} %refs_4_.1, bf16[256,256]{1,0:T(8,128)(2,1)} %refs_5_.1, ...), custom_call_target="tpu_custom_call" | custom-call | tf_op jit(solution)/shard_map/pallas_call | solution.py:426
  98.7 1.6 %shard_map.104 = (f32[1,128]{1,0:T(1,128)}, f32[128,256]{1,0:T(8,128)}, bf16[128,256]{1,0:T(8,128)(2,1)}) custom-call(f32[1,128]{1,0:T(1,128)} %get-tuple-element.9.refs_0_, f32[128,256]{1,0:T(8,128)} %get-tuple-element.10.refs_1_, bf16[128,256]{1,0:T(8,128)(2,1)} %get-tuple-element.11.refs_2_), custom_call_target="tpu_custom_call" | custom-call | tf_op jit(solution)/shard_map/pallas_call | solution.py:443

commit v5 on v4

--- a/solution.py
+++ b/solution.py
@@ -59,7 +59,7 @@
         "un_t": ((NC, NZ, own, bot), BF16),
         "su_tr": ((bot, tok), BF16),
         "di_s": ((nv, rows, bot), BF16),
-        "di_t": ((nv, rows, bot), BF16),
+        "di_t": ((nx, ny, rows, bot), BF16),
         "kf": ((nq, tok, 256), F32),
         "eb": ((tok, nq * 256), BF16),
         "kb": ((tok, nq * 256), BF16),
@@ -78,6 +78,7 @@
         "sc": ((NC, 1, tok), F32),
         "loss": ((tok, 128), F32),
         "cols": ((2, tok, 128), F32),
+        "live": ((tok, 128), F32),
         "lb": ((np_, own, 128), F32),
         "ug": ((NC, 2, half, bot), F32),
         "ur": ((2, half, bot), F32),
@@ -88,7 +89,7 @@
         "bg": ((np_, own, bot), BF16),
     }
     sems = [
-        "zr_s", "zr_t", "cnt", "un_s", "un_t", "uc_s", "uc_t", "di_s", "di_t", "pb0", "pb1", "pb2",
+        "zr_s", "zr_t", "cnt", "un_s", "un_t", "uc_s", "uc_t", "di_s", "dx1", "dy1", "dx2", "dy2", "pb0", "pb1", "pb2",
         "tz0", "tz1", "tc0", "tc1", "ez", "ec", "fz", "fc", "sz", "sc", "lb", "ur", "uz", "rr", "bg",
     ]
     return vmem, sems
@@ -184,21 +185,33 @@
     send_partial("t", th, tb)
     for i in (0, 4, 7, 6, 3):
         loads[i].wait()
+    m["di_t"][x, y] = unit_rows(tp[...].astype(F32))[0].astype(BF16)
+    upper, lower = pl.ds(0, rows // 2), pl.ds(rows // 2, rows // 2)
+    x_peers = [at_v((lax.rem(x + k, nx), y)) for k in range(1, nx)]
+    y_peers = [at_v((x, lax.rem(y + k, ny))) for k in range(1, ny)]
+    for device in x_peers:
+        push("dx1", m["di_t"].at[x, y, upper], m["di_t"].at[x, y, upper], device)
+    for device in y_peers:
+        push("dy1", m["di_t"].at[x, y, lower], m["di_t"].at[x, y, lower], device)
     send_partial("s", sh, sb)
-    m["di_t"][v] = unit_rows(tp[...].astype(F32))[0].astype(BF16)
     m["di_s"][v] = unit_rows(sp[...].astype(F32))[0].astype(BF16)
     m["cnt"][z] = jnp.full((1, 128), count[0].astype(F32), F32)
     to_z("cnt", m["cnt"].at[z], m["cnt"].at[z])
 
     for name in ("t", "s"):
         arrived("zr_" + name, m["zr_" + name].at[pl.ds(0, np_ - 1)])
-        if name == "t":
-            to_v("di_t", m["di_t"].at[v], m["di_t"].at[v])
         own_z = jnp.sum(m["zr_" + name][...], axis=0)
         unit, length = unit_rows(own_z)
         m["un_" + name][c, z] = unit.astype(BF16)
         mine = m["un_" + name].at[c, z]
         to_z("un_" + name, mine, mine)
+        if name == "t":
+            arrived("dx1", m["di_t"].at[pl.ds(0, nx - 1), 0, upper])
+            for device in y_peers:
+                push("dy2", m["di_t"].at[:, y, upper], m["di_t"].at[:, y, upper], device)
+            arrived("dy1", m["di_t"].at[0, pl.ds(0, ny - 1), lower])
+            for device in x_peers:
+                push("dx2", m["di_t"].at[x, :, lower], m["di_t"].at[x, :, lower], device)
         if name == "s":
             m["zown"][...] = own_z
             m["zlen"][...] = jnp.broadcast_to(length, (own, 128))
@@ -213,10 +226,12 @@
     slot = ((y * NC + lane_c) * own + lane_i).astype(F32)
     live = jnp.where(slot < counts, 1.0, 0.0)
 
-    def whole_units(name):
+    def share_units(name):
         arrived("un_" + name, m["un_" + name].at[0, pl.ds(0, NZ - 1)])
         mine = m["un_" + name].at[c]
         push("uc_" + name, mine, mine, sibling)
+
+    def sibling_units(name):
         arrived("uc_" + name, m["un_" + name].at[0])
 
     def units(name):
@@ -225,18 +240,31 @@
     def dirs(name, q):
         return m["di_" + name][pl.ds(2 * q, 2)].reshape(256, bot)
 
-    whole_units("t")
-    arrived("di_t", m["di_t"].at[pl.ds(0, nv - 1)])
-    live_col = twice(column(live))
-
-    def teacher(q, carry):
-        logits = dot_last(units("t"), dirs("t", q))
-        k_tile = live_col * jnp.exp2(logits * (LOG2E / TEACHER_TEMP))
-        m["kf"][q] = k_tile
-        m["pp"][pl.ds(q, 1), :] = jnp.sum(k_tile, axis=0, keepdims=True)
-        return carry
-
-    lax.fori_loop(0, nq, teacher, 0, unroll=4 if nq % 4 == 0 else 1)
+    share_units("t")
+    m["live"][...] = column(live)
+    arrived("dy2", m["di_t"].at[:, pl.ds(0, ny - 1), upper])
+    arrived("dx2", m["di_t"].at[pl.ds(0, nx - 1), :, lower])
+
+    def teacher_dirs(q):
+        return m["di_t"][q // (ny // 2), pl.ds(2 * lax.rem(q, ny // 2), 2)].reshape(256, bot)
+
+    def teacher(side, first):
+        at = pl.ds(pl.multiple_of(side * half, half), half)
+
+        def step(q, carry):
+            logits = dot_last(m["un_t"][side].reshape(half, bot), teacher_dirs(q))
+            k_tile = twice(m["live"][at, :]) * jnp.exp2(logits * (LOG2E / TEACHER_TEMP))
+            m["kf"][q, at, :] = k_tile
+            sums = jnp.sum(k_tile, axis=0, keepdims=True)
+            row = pl.ds(q, 1)
+            m["pp"][row, :] = sums if first else m["pp"][row, :] + sums
+            return carry
+
+        lax.fori_loop(0, nq, step, 0, unroll=nq)
+
+    teacher(c, True)
+    sibling_units("t")
+    teacher(1 - c, False)
 
     def send_p(k):
         part = jnp.concatenate([m["pp"][:, :128], m["pp"][:, 128:]], axis=0)
@@ -288,7 +316,8 @@
         part = m["di_s"].at[v, pl.ds(k * (rows // 2), rows // 2)]
         to_v("di_s", part, part)
         if k == 0:
-            whole_units("s")
+            share_units("s")
+            sibling_units("s")
             m["su_tr"][...] = units("s").astype(F32).T.astype(BF16)
         z_sum("tz%d" % k, "tc%d" % k, z_buf, c_buf)
         total = c_sum("tc%d" % k, c_buf)
@@ -314,6 +343,7 @@
 
     def scaled(q, carry):
         part = m["kf"][q] * m["pv"][pl.ds(q, 1), :]
+        m["kf"][q] = part
         m["kb"][:, pl.ds(pl.multiple_of(q * 256, 256), 256)] = part.astype(BF16)
         return carry
 
@@ -338,15 +368,21 @@
     total_z = c_sum("ec", m["ec"])
     weight = live * (GRAD_SCALE / STUDENT_TEMP) / (counts * images)
     m["cols"][0] = column(weight / total_z)
+    e_col = twice(m["cols"][0])
+
+    def weighted(q, carry):
+        m["ef"][q] = e_col * m["ef"][q]
+        return carry
+
+    lax.fori_loop(0, nq, weighted, 0)
     z_sum("fz", "fc", m["fz"], m["fc"])
     t_row = 1.0 / jnp.where(live > 0, c_sum("fc", m["fc"]), 1.0)
     m["cols"][1] = column(weight * t_row)
 
-    e_col, k_col = twice(m["cols"][0]), twice(m["cols"][1])
+    k_col = twice(m["cols"][1])
 
     def block_grads(q):
-        targets = k_col * (m["kf"][q] * m["pv"][pl.ds(q, 1), :])
-        d_tile = (e_col * m["ef"][q] - targets).astype(BF16)
+        d_tile = (m["ef"][q] - k_col * m["kf"][q]).astype(BF16)
         raw = dot(m["su_tr"][...], d_tile).astype(BF16)
         m["rs"][2 * q] = raw[:, :rows]
         m["rs"][2 * q + 1] = raw[:, rows:]

time: 101 us -> 94.1 us (0.932)
  Pallas kernels: 99 us -> 92.3 us
    pallas_call x1, Pallas kernels: 97.4 us -> 90.7 us  [body(): pl.pallas_call(functools.partial(kernel, d), out_shape=(jax.ShapeDtypeStr...]
where the time goes in v5:
time: 94.1 us; the launch traced here: 93.6 us
  Pallas kernels  92.3 us (98%)
  between operations  1.29 us (1%)
    pallas_call x1, Pallas kernels, body(): pl.pallas_call(functools.partial(kernel, d), out_shape=(jax.ShapeDtypeStr...  90.7 us

profile of v5, /device:TPU:1, one launch (start us, length us, event | category | flops | bytes accessed | tf_op | source)
XLA Modules:
  0.0 93.6 jit_solution(476031602780803038)
XLA Ops:
  1.3 90.7 %shard_map.103 = (f32[1,128]{1,0:T(1,128)}, f32[128,256]{1,0:T(8,128)}, bf16[128,256]{1,0:T(8,128)(2,1)}) custom-call(bf16[256,256]{1,0:T(8,128)(2,1)} %refs_0_.1, bf16[256,256]{1,0:T(8,128)(2,1)} %refs_1_.1, s32[1,128]{1,0:T(1,128)} %refs_2_.1, s32[1]{0:T(128)S(6)} %copy.11.refs_3_, bf16[256,256]{1,0:T(8,128)(2,1)} %refs_4_.1, bf16[256,256]{1,0:T(8,128)(2,1)} %refs_5_.1, ...), custom_call_target="tpu_custom_call" | custom-call | tf_op jit(solution)/shard_map/pallas_call | solution.py:462
  92.0 1.6 %shard_map.104 = (f32[1,128]{1,0:T(1,128)}, f32[128,256]{1,0:T(8,128)}, bf16[128,256]{1,0:T(8,128)(2,1)}) custom-call(f32[1,128]{1,0:T(1,128)} %get-tuple-element.9.refs_0_, f32[128,256]{1,0:T(8,128)} %get-tuple-element.10.refs_1_, bf16[128,256]{1,0:T(8,128)(2,1)} %get-tuple-element.11.refs_2_), custom_call_target="tpu_custom_call" | custom-call | tf_op jit(solution)/shard_map/pallas_call | solution.py:479

commit v6 on v5

--- a/solution.py
+++ b/solution.py
@@ -84,13 +84,19 @@
         "ur": ((2, half, bot), F32),
         "us": ((NZ, 2, own, bot), BF16),
         "uz": ((NZ, 2, own, bot), BF16),
-        "rs": ((nv, bot, rows), BF16),
-        "rr": ((nv, bot, rows), BF16),
+        "xs": ((nx, ny, bot // 2, rows), BF16),
+        "xr": ((nx, ny, bot // 2, rows), BF16),
+        "ys": ((ny, nx, bot // 2, rows), BF16),
+        "yr": ((ny, nx, bot // 2, rows), BF16),
+        "xys": ((ny, bot // 2, rows), BF16),
+        "xyr": ((ny, bot // 2, rows), BF16),
+        "yxs": ((nx, bot // 2, rows), BF16),
+        "yxr": ((nx, bot // 2, rows), BF16),
         "bg": ((np_, own, bot), BF16),
     }
     sems = [
         "zr_s", "zr_t", "cnt", "un_s", "un_t", "uc_s", "uc_t", "di_s", "dx1", "dy1", "dx2", "dy2", "pb0", "pb1", "pb2",
-        "tz0", "tz1", "tc0", "tc1", "ez", "ec", "fz", "fc", "sz", "sc", "lb", "ur", "uz", "rr", "bg",
+        "tz0", "tz1", "tc0", "tc1", "ez", "ec", "fz", "fc", "sz", "sc", "lb", "ur", "uz", "xr", "yr", "xyr", "yxr", "bg",
     ]
     return vmem, sems
 
@@ -380,24 +386,28 @@
     m["cols"][1] = column(weight * t_row)
 
     k_col = twice(m["cols"][1])
-
-    def block_grads(q):
+    pairs = ny // 2
+
+    def block_grads(owner_x, pair):
+        q = owner_x * pairs + pair
         d_tile = (m["ef"][q] - k_col * m["kf"][q]).astype(BF16)
         raw = dot(m["su_tr"][...], d_tile).astype(BF16)
-        m["rs"][2 * q] = raw[:, :rows]
-        m["rs"][2 * q + 1] = raw[:, rows:]
-
-    def send_raw(other):
-        push("rr", m["rs"].at[other], m["rr"].at[v], at_v((other // ny, lax.rem(other, ny))))
-
-    for step in [*range(nq - 1, 0, -1), nq]:
-        q = lax.rem(step + v // 2, nq)
-        block_grads(q)
-        if step < nq:
-            send_raw(2 * q)
-            send_raw(2 * q + 1)
-    send_raw(v + 1 - 2 * lax.rem(v, 2))
-    m["rr"][v] = m["rs"][v]
+        for j in range(2):
+            block = raw[:, j * rows : (j + 1) * rows]
+            m["xs"][owner_x, 2 * pair + j] = block[: bot // 2]
+            m["ys"][2 * pair + j, owner_x] = block[bot // 2 :]
+
+    for step in [*range(nx - 1, 0, -1), 0]:
+        owner_x = lax.rem(x + step, nx)
+        for pair in range(pairs):
+            block_grads(owner_x, pair)
+        if step:
+            push("xr", m["xs"].at[owner_x], m["xr"].at[x], at_v((owner_x, y)))
+    for step in range(ny - 1, 0, -1):
+        owner_y = lax.rem(y + step, ny)
+        push("yr", m["ys"].at[owner_y], m["yr"].at[y], at_v((x, owner_y)))
+    m["xr"][x] = m["xs"][x]
+    m["yr"][y] = m["ys"][y]
 
     z_sum("sz", "sc", m["sz"], m["sc"])
     total_ts = c_sum("sc", m["sc"]) * t_row
@@ -416,13 +426,28 @@
     for other in pr_peers:
         push("bg", m["bg"].at[pr], m["bg"].at[pr], at_pr(other))
 
+    arrived("xr", m["xr"].at[pl.ds(0, nx - 1)])
+    m["xys"][...] = jnp.sum(m["xr"][...].astype(F32), axis=0).astype(BF16)
+    for step in range(ny - 1, 0, -1):
+        owner_y = lax.rem(y + step, ny)
+        push("xyr", m["xys"].at[owner_y], m["xyr"].at[y], at_v((x, owner_y)))
+    m["xyr"][y] = m["xys"][y]
+    arrived("yr", m["yr"].at[pl.ds(0, ny - 1)])
+    m["yxs"][...] = jnp.sum(m["yr"][...].astype(F32), axis=0).astype(BF16)
+    for step in range(nx - 1, 0, -1):
+        owner_x = lax.rem(x + step, nx)
+        push("yxr", m["yxs"].at[owner_x], m["yxr"].at[x], at_v((owner_x, y)))
+    m["yxr"][x] = m["yxs"][x]
+
     arrived("lb", m["lb"].at[pl.ds(0, np_ - 1)])
     loss_out[...] = m["lb"][...].reshape(slots, 128).T[0:1]
     arrived("bg", m["bg"].at[pl.ds(0, np_ - 1)])
     hidden_out[...] = dot_last(m["bg"][...].reshape(slots, bot), sb[...]).astype(BF16)
 
-    arrived("rr", m["rr"].at[pl.ds(0, nv - 1)])
-    raw_grad = jnp.sum(m["rr"][...].astype(F32), axis=0).T
+    arrived("xyr", m["xyr"].at[pl.ds(0, ny - 1)])
+    arrived("yxr", m["yxr"].at[pl.ds(0, nx - 1)])
+    sums = [jnp.sum(m[name][...].astype(F32), axis=0) for name in ("xyr", "yxr")]
+    raw_grad = jnp.concatenate(sums, axis=0).T
     own_raw = sp[...].astype(F32)
     norm = unit_rows(own_raw)[1]
     proto_out[...] = raw_grad / norm - own_raw * jnp.sum(own_raw * raw_grad, axis=1, keepdims=True) / norm**3

time: 94.1 us -> 91.7 us (0.974)
  Pallas kernels: 92.3 us -> 90.2 us
    pallas_call x1, Pallas kernels: 90.7 us -> 88.6 us  [body(): pl.pallas_call(functools.partial(kernel, d), out_shape=(jax.ShapeDtypeStr...]
where the time goes in v6:
time: 91.7 us; the launch traced here: 91.5 us
  Pallas kernels  90.2 us (98%)
  between operations  1.29 us (1%)
    pallas_call x1, Pallas kernels, body(): pl.pallas_call(functools.partial(kernel, d), out_shape=(jax.ShapeDtypeStr...  88.6 us

profile of v6, /device:TPU:1, one launch (start us, length us, event | category | flops | bytes accessed | tf_op | source)
XLA Modules:
  0.0 91.5 jit_solution(16941410935602104117)
XLA Ops:
  1.3 88.6 %shard_map.103 = (f32[1,128]{1,0:T(1,128)}, f32[128,256]{1,0:T(8,128)}, bf16[128,256]{1,0:T(8,128)(2,1)}) custom-call(bf16[256,256]{1,0:T(8,128)(2,1)} %refs_0_.1, bf16[256,256]{1,0:T(8,128)(2,1)} %refs_1_.1, s32[1,128]{1,0:T(1,128)} %refs_2_.1, s32[1]{0:T(128)S(6)} %copy.11.refs_3_, bf16[256,256]{1,0:T(8,128)(2,1)} %refs_4_.1, bf16[256,256]{1,0:T(8,128)(2,1)} %refs_5_.1, ...), custom_call_target="tpu_custom_call" | custom-call | tf_op jit(solution)/shard_map/pallas_call | solution.py:487
  89.9 1.6 %shard_map.104 = (f32[1,128]{1,0:T(1,128)}, f32[128,256]{1,0:T(8,128)}, bf16[128,256]{1,0:T(8,128)(2,1)}) custom-call(f32[1,128]{1,0:T(1,128)} %get-tuple-element.9.refs_0_, f32[128,256]{1,0:T(8,128)} %get-tuple-element.10.refs_1_, bf16[128,256]{1,0:T(8,128)(2,1)} %get-tuple-element.11.refs_2_), custom_call_target="tpu_custom_call" | custom-call | tf_op jit(solution)/shard_map/pallas_call | solution.py:504
